TPU v7x, 32 devices: a whole 2x2x4 slice. The times are simulated.
32 devices in a mesh: dp: 8 (over z, x), mp: 4 (over y, core).
Axes of the slice: x: 2, y: 2, z: 4, core: 2. Of those that a mesh axis runs over, the one named last changes fastest.
Arguments:
- owner: int32 [16384, 1], P(('dp', 'mp')), may hold values from 0 to 7; in each aligned block of 512 rows (0 to 511, 512 to 1023, ...) at most 256 rows name the same one
- slot: int32 [16384], P(('dp', 'mp')), may hold values from 0 to 8191
- table: bfloat16 [65536, 512], P('dp'), may hold values from -6 to 6
- w_in1: bfloat16 [512, 8, 256], P(None, None, 'mp'), may hold values from -0.25 to 0.25
- b_in1: bfloat16 [8, 256], P(None, 'mp'), may hold values from -4 to 4
- w_out1: bfloat16 [8, 256, 256], P(None, 'mp'), may hold values from -0.375 to 0.375
- b_out1: bfloat16 [8, 256], replicated, may hold values from -0.75 to 0.75
- gate1: bfloat16 [512, 2, 8], replicated, may hold values from -0.125 to 0.125
- w_in2: bfloat16 [512, 8, 256], P(None, None, 'mp'), may hold values from -0.25 to 0.25
- b_in2: bfloat16 [8, 256], P(None, 'mp'), may hold values from -4 to 4
- w_out2: bfloat16 [8, 256, 256], P(None, 'mp'), may hold values from -0.375 to 0.375
- b_out2: bfloat16 [8, 256], replicated, may hold values from -0.75 to 0.75
- gate2: bfloat16 [512, 3, 8], replicated, may hold values from -0.25 to 0.25
- tower_in: bfloat16 [3, 256, 128], replicated, may hold values from -0.375 to 0.375
- tower_bias: bfloat16 [3, 128], replicated, may hold values from -4 to 4
- tower_out: bfloat16 [3, 128], replicated, may hold values from -0.5 to 0.5
- tower_out_bias: bfloat16 [3], replicated, may hold values from -4 to 4
- pred_cot: float32 [3, 16384], P(None, ('dp', 'mp')), may hold values from -6 to 6
Outputs:
- predictions: float32 [3, 16384], P(None, ('dp', 'mp'))
- table_grad: float32 [65536, 512], P('dp', 'mp')
- w_in1_grad: float32 [512, 8, 256], P(None, None, 'mp')
- b_in1_grad: float32 [8, 256], P(None, 'mp')
- w_out1_grad: float32 [8, 256, 256], P(None, 'mp')
- b_out1_grad: float32 [8, 256], replicated
- gate1_grad: float32 [512, 2, 8], replicated
- w_in2_grad: float32 [512, 8, 256], P(None, None, 'mp')
- b_in2_grad: float32 [8, 256], P(None, 'mp')
- w_out2_grad: float32 [8, 256, 256], P(None, 'mp')
- b_out2_grad: float32 [8, 256], replicated
- gate2_grad: float32 [512, 3, 8], replicated
- tower_in_grad: float32 [3, 256, 128], replicated
- tower_bias_grad: float32 [3, 128], replicated
- tower_out_grad: float32 [3, 128], replicated
- tower_out_bias_grad: float32 [3], replicated
Inputs may be any that keep to these rules, and one draw needn't show every extreme that they name: Among the 512 rows of one device no owner is named by more than 256 rows, and in some devices' rows one owner by exactly 256.
All inputs are finite; a program needn't handle non-finite values.
Results may differ from a plain program's by a relative error of at most 0.025.
Values may be sent and summed in bfloat16 or wider, within the bound.
A program may use at most 128 MiB of HBM per device.

v0:
```python
import jax
import jax.numpy as jnp
from jax import lax
from jax.sharding import PartitionSpec as P


def silu_slope(values):
    sig = jax.nn.sigmoid(values)
    return sig * (1.0 + values * (1.0 - sig))


def layer_forward(inputs, w_in, b_in, w_out, b_out, gate):
    rows, width = inputs.shape
    experts, eout = b_out.shape
    inner = w_in.shape[2]
    tasks = gate.shape[1]
    flat_gate = gate.reshape(width, -1)
    pre = jnp.dot(inputs, w_in.reshape(width, -1), preferred_element_type=jnp.float32)
    pre = pre + b_in.reshape(-1).astype(jnp.float32)
    hidden = jax.nn.silu(pre).astype(jnp.bfloat16)
    grouped = hidden.reshape(-1, experts, inner)
    logits = jnp.dot(inputs, flat_gate, preferred_element_type=jnp.float32)
    weights = jax.nn.softmax(logits.reshape(rows, tasks, experts), axis=-1)
    weights_whole = None
    summed = jnp.einsum("rek,ekd->red", grouped, w_out, preferred_element_type=jnp.float32)
    outputs = summed + b_out.astype(jnp.float32)
    mixed = jnp.einsum("rte,red->rtd", weights, outputs)
    return (mixed, (inputs, pre, hidden, outputs, weights, weights_whole))


def layer_backward(grad_mixed, inputs, w_in, w_out, gate, saved):
    whole, pre, hidden, outputs, weights, weights_whole = saved
    rows, width = inputs.shape
    experts = w_out.shape[0]
    inner = w_in.shape[2]
    grad_out = jnp.einsum("rte,rtd->red", weights, grad_mixed).astype(jnp.bfloat16)
    grad_weights = jnp.einsum("rtd,red->rte", grad_mixed, outputs)
    centred = grad_weights - jnp.sum(weights * grad_weights, axis=-1, keepdims=True)
    grad_logits = (weights * centred).astype(jnp.bfloat16).reshape(rows, -1)
    flat_gate = gate.reshape(width, -1)
    gate_grad = jnp.einsum("ri,rj->ij", inputs, grad_logits, preferred_element_type=jnp.float32)
    gate_grad = gate_grad.reshape(gate.shape)
    input_from_gate = jnp.einsum(
        "rj,ij->ri", grad_logits, flat_gate, preferred_element_type=jnp.float32
    )
    out_bias_grad = jnp.sum(grad_out, axis=0, dtype=jnp.float32)
    grouped = hidden.reshape(-1, experts, inner)
    w_out_grad = jnp.einsum("rek,red->ekd", grouped, grad_out, preferred_element_type=jnp.float32)
    grad_hidden = jnp.einsum("red,ekd->rek", grad_out, w_out, preferred_element_type=jnp.float32)
    grad_pre = (grad_hidden.reshape(-1, experts * inner) * silu_slope(pre)).astype(jnp.bfloat16)
    in_bias_grad = jnp.sum(grad_pre, axis=0, dtype=jnp.float32).reshape(experts, inner)
    w_in_grad = jnp.einsum("ri,rj->ij", whole, grad_pre, preferred_element_type=jnp.float32)
    w_in_grad = w_in_grad.reshape(w_in.shape)
    flat_w = w_in.reshape(width, -1)
    input_grad = jnp.einsum("rj,ij->ri", grad_pre, flat_w, preferred_element_type=jnp.float32)
    input_grad = input_grad + input_from_gate
    return (input_grad, (w_in_grad, in_bias_grad, w_out_grad), (out_bias_grad, gate_grad))


def on_device(
    owner,
    slot,
    table,
    w_in1,
    b_in1,
    w_out1,
    b_out1,
    gate1,
    w_in2,
    b_in2,
    w_out2,
    b_out2,
    gate2,
    tower_in,
    tower_bias,
    tower_out,
    tower_out_bias,
    pred_cot,
):
    count_dp = lax.axis_size("dp")
    rows = owner.shape[0]
    width = table.shape[1]
    capacity = 4 * rows // count_dp
    target = owner[:, 0]
    onehot = (target[:, None] == jnp.arange(count_dp, dtype=jnp.int32)[None, :]).astype(jnp.int32)
    before = jnp.cumsum(onehot, axis=0) - onehot
    rank = jnp.sum(before * onehot, axis=1)
    place = target * capacity + rank
    request = jnp.zeros((count_dp * capacity,), jnp.int32).at[place].set(slot)
    wanted = lax.all_to_all(
        request.reshape(count_dp, capacity), "dp", split_axis=0, concat_axis=0, tiled=True
    )
    wanted = wanted.reshape(count_dp * capacity)
    served = jnp.take(table, wanted, axis=0).reshape(count_dp, capacity, width)
    fetched = lax.all_to_all(served, "dp", split_axis=0, concat_axis=0, tiled=True).reshape(
        count_dp * capacity, width
    )
    embedded = jnp.take(fetched, place, axis=0)
    w_in1, b_in1, w_out1, w_in2, b_in2, w_out2 = (
        lax.all_gather(w_in1, "mp", axis=2, tiled=True),
        lax.all_gather(b_in1, "mp", axis=1, tiled=True),
        lax.all_gather(w_out1, "mp", axis=1, tiled=True),
        lax.all_gather(w_in2, "mp", axis=2, tiled=True),
        lax.all_gather(b_in2, "mp", axis=1, tiled=True),
        lax.all_gather(w_out2, "mp", axis=1, tiled=True),
    )
    mixed_one, saved_one = layer_forward(embedded, w_in1, b_in1, w_out1, b_out1, gate1)
    second = jnp.concatenate([mixed_one[:, 0, :], mixed_one[:, 1, :]], axis=-1).astype(jnp.bfloat16)
    mixed_two, saved_two = layer_forward(second, w_in2, b_in2, w_out2, b_out2, gate2)
    rounded = mixed_two.astype(jnp.bfloat16)
    act = jnp.einsum("rtd,tdk->rtk", rounded, tower_in, preferred_element_type=jnp.float32)
    act = act + tower_bias.astype(jnp.float32)
    smooth = jax.nn.silu(act)
    out_weights = tower_out.astype(jnp.float32)
    logit = jnp.sum(smooth * out_weights, axis=-1) + tower_out_bias.astype(jnp.float32)
    prob = jax.nn.sigmoid(logit)
    predictions = prob.T
    grad_logit = pred_cot.T * prob * (1.0 - prob)
    tower_out_bias_grad = jnp.sum(grad_logit, axis=0)
    tower_out_grad = jnp.einsum("rt,rtk->tk", grad_logit, smooth)
    grad_act = (grad_logit[:, :, None] * out_weights * silu_slope(act)).astype(jnp.bfloat16)
    tower_bias_grad = jnp.sum(grad_act, axis=0, dtype=jnp.float32)
    tower_in_grad = jnp.einsum(
        "rtd,rtk->tdk", rounded, grad_act, preferred_element_type=jnp.float32
    )
    grad_mixed_two = jnp.einsum(
        "rtk,tdk->rtd", grad_act, tower_in, preferred_element_type=jnp.float32
    )
    grad_second, sharded_two, shared_two = layer_backward(
        grad_mixed_two, second, w_in2, w_out2, gate2, saved_two
    )
    eout = b_out1.shape[1]
    grad_mixed_one = grad_second.reshape(rows, 2, eout)
    grad_first, sharded_one, shared_one = layer_backward(
        grad_mixed_one, embedded, w_in1, w_out1, gate1, saved_one
    )
    sendback = jnp.zeros((count_dp * capacity, width), jnp.float32).at[place].set(grad_first)
    arrived = lax.all_to_all(
        sendback.reshape(count_dp, capacity, width), "dp", split_axis=0, concat_axis=0, tiled=True
    )
    arrived = arrived.reshape(count_dp * capacity, width)
    table_part = jnp.zeros((table.shape[0], width), jnp.float32).at[wanted].add(arrived)
    table_grad = lax.psum_scatter(table_part, "mp", scatter_dimension=1, tiled=True)
    sharded = (
        sharded_one[0],
        sharded_one[1],
        sharded_one[2],
        sharded_two[0],
        sharded_two[1],
        sharded_two[2],
    )
    sharded = (
        lax.psum_scatter(sharded[0], "mp", scatter_dimension=2, tiled=True),
        lax.psum_scatter(sharded[1], "mp", scatter_dimension=1, tiled=True),
        lax.psum_scatter(sharded[2], "mp", scatter_dimension=1, tiled=True),
        lax.psum_scatter(sharded[3], "mp", scatter_dimension=2, tiled=True),
        lax.psum_scatter(sharded[4], "mp", scatter_dimension=1, tiled=True),
        lax.psum_scatter(sharded[5], "mp", scatter_dimension=1, tiled=True),
    )
    summed = lax.psum(
        (sharded[0], sharded[1], sharded[2], sharded[3], sharded[4], sharded[5]), "dp"
    )
    shared = lax.psum(
        (
            shared_one[0],
            shared_one[1],
            shared_two[0],
            shared_two[1],
            tower_in_grad,
            tower_bias_grad,
            tower_out_grad,
            tower_out_bias_grad,
        ),
        ("dp", "mp"),
    )
    return (
        predictions,
        table_grad,
        summed[0],
        summed[1],
        summed[2],
        shared[0],
        shared[1],
        summed[3],
        summed[4],
        summed[5],
        shared[2],
        shared[3],
        shared[4],
        shared[5],
        shared[6],
        shared[7],
    )


def solution(mesh):
    in_specs = (
        P(("dp", "mp"), None),
        P(("dp", "mp")),
        P("dp", None),
        P(None, None, "mp"),
        P(None, "mp"),
        P(None, "mp", None),
        P(),
        P(),
        P(None, None, "mp"),
        P(None, "mp"),
        P(None, "mp", None),
        P(),
        P(),
        P(),
        P(),
        P(),
        P(),
        P(None, ("dp", "mp")),
    )
    out_specs = (
        P(None, ("dp", "mp")),
        P("dp", "mp"),
        P(None, None, "mp"),
        P(None, "mp"),
        P(None, "mp", None),
        P(),
        P(),
        P(None, None, "mp"),
        P(None, "mp"),
        P(None, "mp", None),
        P(),
        P(),
        P(),
        P(),
        P(),
        P(),
    )
    return jax.shard_map(
        on_device, mesh=mesh, in_specs=in_specs, out_specs=out_specs, check_vma=False
    )
```

profile of v0, /device:TPU:1, one launch (start us, length us, event | category | flops | bytes accessed | tf_op | source)
XLA Modules:
  0.0 883.7 jit_solution(3995728132606353996)
XLA Ops:
  14.7 6.4 all-to-all-start
  21.8 4.6 all-to-all-done
  26.4 12.1 %gather_fusion = bf16[2048,512]{1,0:T(8,128)(2,1)S(1)} fusion(bf16[8192,512]{1,0:T(8,128)(2,1)} %param.20, s32[2048]{0:T(1024)S(1)} %broadcast_clamp_fusion), kind=kCustom, calls=%fused_computation | custom fusion | bytes 4202496 | tf_op jit(solution)/shard_map/jit(_take)/gather | solution.py:94
  46.3 7.0 all-gather
  53.5 5.7 all-gather.1
  59.3 30.7 %all-to-all-done.1 = bf16[8,256,512]{2,1,0:T(8,128)(2,1)S(1)} async-done(((bf16[8,256,512]{2,1,0:T(8,128)(2,1)}), bf16[8,256,512]{2,1,0:T(8,128)(2,1)S(1)}, u32[]{:S(2)}, u32[]{:S(2)}) %all-to-all-start.1) | async-done | bytes 2097184 | tf_op jit(solution)/shard_map/all_to_all | solution.py:95
  92.7 6.0 multiply_convert_fusion.3
  106.9 5.9 multiply_convert_fusion.2
  132.6 4.6 fusion.4
  138.6 4.9 fusion.26
  143.5 5.6 copy.196
  149.1 4.8 convert_reduce_fusion.1
  166.7 5.4 copy.197
  172.1 4.9 convert_reduce_fusion.3
  198.5 5.8 all-to-all-start.2
  211.6 34.9 %reduce-scatter.14.cloned.1.call-done = f32[512,8,64]{0,2,1:T(8,128)} async-done(((f32[512,8,256]{0,2,1:T(8,128)}), f32[512,8,64]{0,2,1:T(8,128)}) %reduce-scatter.14.cloned.1.call-update) | async-done | bytes 1048592 | tf_op jit(solution)/shard_map/reduce_scatter | solution.py:153
  246.5 47.2 %reduce-scatter.18.cloned.1.call-done = f32[512,8,64]{0,2,1:T(8,128)} async-done(((f32[512,8,256]{0,2,1:T(8,128)}), f32[512,8,64]{0,2,1:T(8,128)}) %reduce-scatter.18.cloned.1.call-update) | async-done | bytes 1048592 | tf_op jit(solution)/shard_map/reduce_scatter | solution.py:156
  296.4 21.7 %scatter_custom_fusion.2 = f32[8192,512]{1,0:T(8,128)} fusion(s32[2048]{0:T(1024)S(1)} %bitcast.194, f32[2048,512]{1,0:T(8,128)} %bitcast.41, f32[]{:T(128)} %constant.34.clone.1), kind=kCustom, calls=%fused_computation.7 | custom fusion | flops 1048576 | bytes 16777728 | tf_op jit(solution)/shard_map/scatter-add | solution.py:142
  319.0 19.6 %reduce-scatter.22.cloned.1.call-done = f32[64,8]{1,0:T(8,128)} async-done(((f32[256,8]{1,0:T(8,128)}), f32[64,8]{1,0:T(8,128)}) %reduce-scatter.22.cloned.1.call-update) | async-done | bytes 2064
  339.3 18.4 %all-reduce.1 = (f32[8,64]{1,0:T(8,128)}, f32[8,64]{1,0:T(8,128)}) all-reduce(f32[8,64]{1,0:T(8,128)S(1)} %copy.201, f32[8,64]{1,0:T(8,128)S(1)} %copy.203), channel_id=1, replica_groups=mesh['dp'=8,'mp'=4] {'dp'}, use_global_device_ids=true, to_apply=%region_18.19 | all-reduce | flops 1024 | bytes 8192 | tf_op jit(solution)/shard_map/psum | solution.py:160
  357.7 112.6 %all-reduce.9.cloned.1.call-done = (f32[8,256]{1,0:T(8,128)}, f32[512,2,8]{0,2,1:T(8,128)}, f32[8,256]{1,0:T(8,128)}, f32[512,3,8]{0,2,1:T(8,128)}, f32[3,128]{1,0:T(4,128)}, /*index=5*/f32[3,128]{1,0:T(4,128)}, f32[3]{0:T(128)}) async-done(((f32[8,256]{1,0:T(8,128)}, f32[512,2,8]{0,2,1:T(8,128)}, f32[8,256]{1,0:T(8,128)}, f32[512,3,8]{0,2,1:T(8,128)}, f32[3,128]{1,0:T(4,128)}, ...) | async-done | bytes 101404 | tf_op jit(solution)/shard_map/psum | solution.py:163
  470.3 134.4 %all-reduce.7.cloned.1.call-done = f32[3,256,128]{2,1,0:T(8,128)} async-done(((f32[3,256,128]{2,1,0:T(8,128)}), f32[3,256,128]{2,1,0:T(8,128)}) %all-reduce.7.cloned.1.call-update) | async-done | bytes 393232 | tf_op jit(solution)/shard_map/psum | solution.py:163
  604.7 134.1 %all-reduce.11.cloned.1.call-done = (f32[512,8,64]{0,2,1:T(8,128)}, f32[8,64,256]{2,1,0:T(8,128)}, f32[512,8,64]{0,2,1:T(8,128)}, f32[8,64,256]{2,1,0:T(8,128)}) async-done(((f32[512,8,64]{0,2,1:T(8,128)}, f32[8,64,256]{2,1,0:T(8,128)}, f32[512,8,64]{0,2,1:T(8,128)}, f32[8,64,256]{2,1,0:T(8,128)}), (f32[512,8,64]{0,2,1:T(8,128)}, f32[8,64,256]{2,1,0:T(8,128)}, f32[512,8,64]{0,2,1:T(8,128)}, ...) | async-done | bytes 3145744 | tf_op jit(solution)/shard_map/psum | solution.py:160
  738.8 128.3 %reduce-scatter.12.cloned.1.call-done = f32[8192,128]{1,0:T(8,128)} async-done(((f32[8192,512]{1,0:T(8,128)}), f32[8192,128]{1,0:T(8,128)}) %reduce-scatter.12.cloned.1.call-update) | async-done | bytes 4194320 | tf_op jit(solution)/shard_map/reduce_scatter | solution.py:143
  (229 shorter events, 103.3 us)
Async XLA Ops:
  7.2 114.0 %copy-start = (bf16[3,256,128]{2,1,0:T(8,128)(2,1)S(1)}, bf16[3,256,128]{2,1,0:T(8,128)(2,1)}, u32[]{:S(2)}) copy-start(bf16[3,256,128]{2,1,0:T(8,128)(2,1)} %param.31) | copy-start | bytes 589828
  7.2 85.5 %all-gather.7.cloned.1.call-start = ((), (), s32[]{:S(2)}) async-start(), calls=%async_computation.10 | async-start | bytes 2621440 | tf_op jit(solution)/shard_map/all_gather | solution.py:100
  14.7 11.7 %all-to-all-start = ((s32[8,1,256]{2,1,0:T(1,128)}), s32[8,1,256]{2,1,0:T(1,128)S(1)}, u32[]{:S(2)}, u32[]{:S(2)}) async-start(s32[8,1,256]{2,1,0:T(1,128)} %bitcast.6), calls=%async_computation | async-start | bytes 16384 | tf_op jit(solution)/shard_map/all_to_all | solution.py:90
  21.0 80.6 %all-gather.9.cloned.1.call-start = ((), (), s32[]{:S(2)}) async-start(), calls=%async_computation.11 | async-start | bytes 1310720 | tf_op jit(solution)/shard_map/all_gather | solution.py:102
  40.1 13.4 %copy-start.43 = (bf16[8,64]{1,0:T(8,128)(2,1)S(1)}, bf16[8,64]{1,0:T(8,128)(2,1)}, u32[]{:S(2)}) copy-start(bf16[8,64]{1,0:T(8,128)(2,1)} %param.27) | copy-start | bytes 3076
  40.1 19.2 %copy-start.41 = (bf16[8,256]{1,0:T(8,128)(2,1)S(1)}, bf16[8,256]{1,0:T(8,128)(2,1)}, u32[]{:S(2)}) copy-start(bf16[8,256]{1,0:T(8,128)(2,1)} %param.29) | copy-start | bytes 12292
  40.1 49.9 %all-to-all-start.1 = ((bf16[8,256,512]{2,1,0:T(8,128)(2,1)}), bf16[8,256,512]{2,1,0:T(8,128)(2,1)S(1)}, u32[]{:S(2)}, u32[]{:S(2)}) async-start(bf16[8,256,512]{2,1,0:T(8,128)(2,1)} %broadcast_select_fusion), calls=%async_computation.1 | async-start | bytes 4194304 | tf_op jit(solution)/shard_map/all_to_all | solution.py:95
  43.9 63.0 %all-gather.11.cloned.1.call-start = ((), (), s32[]{:S(2)}) async-start(), calls=%async_computation.12 | async-start | bytes 2621440 | tf_op jit(solution)/shard_map/all_gather | solution.py:103
  44.6 72.3 %all-gather.13.cloned.1.call-start = ((), (), s32[]{:S(2)}) async-start(), calls=%async_computation.13 | async-start | bytes 1310720 | tf_op jit(solution)/shard_map/all_gather | solution.py:105
  45.2 166.4 %reduce-scatter.20.cloned.1.call-start = ((), (), s32[]{:S(2)}) async-start(), calls=%async_computation.18 | async-start | bytes 2621440 | tf_op jit(solution)/shard_map/reduce_scatter | solution.py:158
  132.5 79.1 %reduce-scatter.16.cloned.1.call-start = ((), (), s32[]{:S(2)}) async-start(), calls=%async_computation.16 | async-start | bytes 2621440 | tf_op jit(solution)/shard_map/reduce_scatter | solution.py:155
  162.2 84.3 %reduce-scatter.14.cloned.1.call-start = ((), (), s32[]{:S(2)}) async-start(), calls=%async_computation.15 | async-start | bytes 5242880 | tf_op jit(solution)/shard_map/reduce_scatter | solution.py:153
  180.3 113.4 %reduce-scatter.18.cloned.1.call-start = ((), (), s32[]{:S(2)}) async-start(), calls=%async_computation.17 | async-start | bytes 5242880 | tf_op jit(solution)/shard_map/reduce_scatter | solution.py:156
  198.5 97.9 %all-to-all-start.2 = ((f32[8,256,512]{2,1,0:T(8,128)}), f32[8,256,512]{2,1,0:T(8,128)}, u32[]{:S(2)}, u32[]{:S(2)}) async-start(f32[8,256,512]{2,1,0:T(8,128)} %bitcast.177), calls=%async_computation.2 | async-start | bytes 8388608 | tf_op jit(solution)/shard_map/all_to_all | solution.py:138
  204.3 113.8 %reduce-scatter.24.cloned.1.call-start = ((), (), s32[]{:S(2)}) async-start(), calls=%async_computation.21 | async-start | bytes 163840
  205.2 133.3 %reduce-scatter.22.cloned.1.call-start = ((), (), s32[]{:S(2)}) async-start(), calls=%async_computation.20 | async-start | bytes 163840
  206.1 264.2 %all-reduce.9.cloned.1.call-start = ((), (), s32[]{:S(2)}) async-start(), calls=%async_computation.22 | async-start | bytes 205824 | tf_op jit(solution)/shard_map/psum | solution.py:163
  210.3 394.4 %all-reduce.7.cloned.1.call-start = ((), (), s32[]{:S(2)}) async-start(), calls=%async_computation.19 | async-start | bytes 786432 | tf_op jit(solution)/shard_map/psum | solution.py:163
  211.5 527.3 %all-reduce.11.cloned.1.call-start = ((), (), s32[]{:S(2)}) async-start(), calls=%async_computation.23 | async-start | bytes 6291456 | tf_op jit(solution)/shard_map/psum | solution.py:160
  293.8 573.4 %reduce-scatter.12.cloned.1.call-start = ((), (), s32[]{:S(2)}) async-start(), calls=%async_computation.14 | async-start | bytes 20971520 | tf_op jit(solution)/shard_map/reduce_scatter | solution.py:143
  470.3 399.9 %copy-start.38 = (f32[8,256]{1,0:T(8,128)S(1)}, f32[8,256]{1,0:T(8,128)}, u32[]{:S(2)}) copy-start(f32[8,256]{1,0:T(8,128)} %get-tuple-element.63) | copy-start | bytes 24580
  470.3 400.5 %copy-start.33 = (f32[512,2,8]{0,2,1:T(8,128)S(1)}, f32[512,2,8]{0,2,1:T(8,128)}, u32[]{:S(2)}) copy-start(f32[512,2,8]{0,2,1:T(8,128)} %get-tuple-element.64) | copy-start | bytes 98308
  738.8 130.6 %copy-start.28 = (f32[8,64,256]{2,1,0:T(8,128)S(1)}, f32[8,64,256]{2,1,0:T(8,128)}, u32[]{:S(2)}) copy-start(f32[8,64,256]{2,1,0:T(8,128)} %get-tuple-element.62) | copy-start | bytes 1572868
  738.8 132.6 %copy-start.20 = (f32[512,8,64]{0,2,1:T(8,128)S(1)}, f32[512,8,64]{0,2,1:T(8,128)}, u32[]{:S(2)}) copy-start(f32[512,8,64]{0,2,1:T(8,128)} %get-tuple-element.65) | copy-start | bytes 3145732
  (46 other events, 180.5 us)
Sparse Core Ops, SparseCore 0:
  9.6 25.0 all-gather.6
  36.3 16.7 all-gather.8
  54.6 22.5 all-gather.10
  78.6 16.7 all-gather.12
  132.6 32.7 reduce-scatter.19
  168.0 31.4 reduce-scatter.15
  202.0 44.4 reduce-scatter.13
  249.2 44.5 reduce-scatter.17
  296.8 19.1 reduce-scatter.23
  318.9 19.5 reduce-scatter.21
  346.1 124.1 all-reduce.8
  476.9 127.7 all-reduce.6
  608.6 130.2 all-reduce.10
  742.0 125.0 reduce-scatter.11
where the time goes:
time: 889 us; the launch traced here: 884 us
  waiting for transfers between devices  652 us (73%)
  local copies, waits for them, and re-layouts  65 us (7%)
  matrix products  64.1 us (7%)
  other arithmetic  39.9 us (4%)
  blocking collectives  31.1 us (3%)
  starting transfers between devices  16.8 us (2%)
  between operations  14.9 us (2%)
    psum x2, waiting for transfers between devices, on_device(): lax.psum((shared_one[0], shared_one[1], shared_two[0], shared_two[1], tow...  247 us
    psum x1, waiting for transfers between devices, on_device(): lax.psum((sharded[0], sharded[1], sharded[2], sharded[3], sharded[4], sha...  134 us
    reduce_scatter x1, waiting for transfers between devices, on_device(): lax.psum_scatter(table_part, 'mp', scatter_dimension=1, tiled=True)  128 us
    reduce_scatter x1, waiting for transfers between devices, on_device(): lax.psum_scatter(sharded[3], 'mp', scatter_dimension=2, tiled=True)  47.2 us
    reduce_scatter x1, waiting for transfers between devices, on_device(): lax.psum_scatter(sharded[0], 'mp', scatter_dimension=2, tiled=True)  34.9 us
    all_to_all x1, waiting for transfers between devices, on_device(): lax.all_to_all(served, 'dp', split_axis=0, concat_axis=0, tiled=True)  30.7 us
    unnamed x16, waiting for transfers between devices  22.3 us
    scatter-add x1, other arithmetic, on_device(): jnp.zeros((table.shape[0], width), jnp.float32).at[wanted].add(arrived)  21.7 us
  transfers between devices with their start and end apart: 17, of which 10 were waited for; matrix products, arithmetic and copies ran while one was open for 16% of the time, Pallas kernels for 0%

commit v1 on v0

v1 whole, which is shorter than its diff:
```python
import functools

import jax
import jax.numpy as jnp
from jax import lax
from jax.experimental import pallas as pl
from jax.experimental.pallas import tpu as pltpu
from jax.sharding import PartitionSpec as P

F32, BF16 = jnp.float32, jnp.bfloat16
MESH = pl.DeviceIdType.MESH
MIB = 2**20
VMEM, ANY = pltpu.VMEM, pl.ANY
NN, NT, TN = ((1,), (0,)), ((1,), (1,)), ((0,), (0,))


def dot(a, b, dims=NN):
    return lax.dot_general(a, b, (dims, ((), ())), preferred_element_type=F32)


def remote(src, dst, send_sem, recv_sem, device):
    return pltpu.make_async_remote_copy(
        src_ref=src,
        dst_ref=dst,
        send_sem=send_sem,
        recv_sem=recv_sem,
        device_id=device,
        device_id_type=MESH,
    )


def greet(peers):
    barrier = pltpu.get_barrier_semaphore()
    for peer in peers:
        pl.semaphore_signal(barrier, inc=1, device_id=peer, device_id_type=MESH)
    pl.semaphore_wait(barrier, len(peers))


def partners(n_dp):
    d, p = lax.axis_index("dp"), lax.axis_index("mp")
    return d, p, p + 1 - 2 * (p % 2), (p + 2) % 4, d + 1 - 2 * (d % 2)


def fetch_kernel(
    n_dp, cap, owner, slot, cot, ws1, ws2, table,
    x_t, req, place_out, wa1, wa2,
    send, recv, idx_v, idx_s, stage, tab, xbuf,
    own_sem, ag_send, ag_recv, rq_send, rq_recv, idx_sem, tab_sem,
):
    d, p, p1, p2, d1 = partners(n_dp)
    rows = owner.shape[1]
    half = ws1.shape[0] // 2
    dx = d % 2
    blocks = table.shape[0] // stage.shape[1]
    step = stage.shape[1]

    def load(b):
        return pltpu.make_async_copy(
            table.at[pl.ds(b * step, step)], stage.at[b % 2], tab_sem.at[b % 2]
        )

    for b in range(min(2, blocks)):
        load(b).start()

    greet([((d + k) % n_dp, p) for k in range(1, n_dp)] + [(d, p1), (d, p2)])

    shards, wholes = (ws1, ws2), (wa1, wa2)
    own, core, across = [], [], []
    for layer in range(2):
        ws, wa = shards[layer], wholes[layer]
        own.append(pltpu.make_async_copy(ws, wa.at[p], own_sem.at[layer]))
        core.append(
            remote(ws, wa.at[p], ag_send.at[layer, 0], ag_recv.at[layer, 0], (d, p1))
        )
        mine = pl.ds(half * dx, half)
        across.append(
            remote(
                ws.at[mine], wa.at[p, mine], ag_send.at[layer, 1], ag_recv.at[layer, 1], (d, p2)
            )
        )
        across[layer].start()
        own[layer].start()
        core[layer].start()

    own_row = owner[...]
    count = max(8, n_dp)
    ks = lax.broadcasted_iota(jnp.int32, (count, rows), 0)
    onehot = jnp.where(ks == own_row, 1.0, 0.0)
    upper = jnp.where(
        lax.broadcasted_iota(jnp.int32, (rows, rows), 0)
        < lax.broadcasted_iota(jnp.int32, (rows, rows), 1),
        1.0,
        0.0,
    ).astype(BF16)
    before = dot(onehot.astype(BF16), upper)
    rank = jnp.sum(before * onehot, axis=0, keepdims=True).astype(jnp.int32)
    place = own_row * cap + rank
    place_out[...] = place
    slots = slot[...]
    c = cot[...]
    high = c.astype(BF16).astype(F32)
    mid = (c - high).astype(BF16).astype(F32)
    low = c - high - mid
    payload = jnp.concatenate(
        [
            (slots // 128).astype(F32),
            (slots % 128).astype(F32),
            high,
            mid,
            low,
            jnp.zeros((16 - 11, rows), F32),
        ],
        axis=0,
    ).astype(BF16)
    for k in range(n_dp):
        at = lax.broadcasted_iota(jnp.int32, (cap, rows), 0) + k * cap
        pick = jnp.where(at == place, 1.0, 0.0).astype(BF16)
        got = dot(payload, pick, NT)
        send[k] = jnp.concatenate(
            [
                got[0:1] * 128.0 + got[1:2],
                got[2:5] + got[5:8] + got[8:11],
                jnp.zeros((4, cap), F32),
            ],
            axis=0,
        )
    asks = []
    for k in range(1, n_dp):
        to = (d + k) % n_dp
        asks.append(
            remote(send.at[to], recv.at[d], rq_send.at[k], rq_recv.at[k], (to, p))
        )
        asks[-1].start()
    recv[d] = send[d]

    def widen(b, carry):
        load(b).wait()
        tab[pl.ds(pl.multiple_of(b * step, step), step), :] = stage[b % 2].astype(F32)

        @pl.when(b + 2 < blocks)
        def _():
            load(b + 2).start()

        return carry

    lax.fori_loop(0, blocks, widen, 0)

    for ask in asks:
        ask.wait()
    for i in range(n_dp):
        got = recv[i]
        idx_v[i : i + 1, :] = jnp.clip(got[0:1].astype(jnp.int32), 0, table.shape[0] - 1)
        req[i] = got
    to_smem = pltpu.make_async_copy(idx_v, idx_s, idx_sem)
    to_smem.start()
    to_smem.wait()

    onward, spread, late = [None] * 2, [None] * 2, [None] * 2

    def forward(layer):
        wa = wholes[layer]
        part = wa.at[p2, pl.ds(half * dx, half)]
        across[layer].wait_recv()
        onward[layer] = remote(
            part, part, ag_send.at[layer, 2], ag_recv.at[layer, 2], (d1, p)
        )
        spread[layer] = remote(
            part, part, ag_send.at[layer, 3], ag_recv.at[layer, 3], (d, p1)
        )
        onward[layer].start()
        spread[layer].start()

    span = xbuf.shape[0]
    total = n_dp * cap
    for j in range(total // span):

        def fill(o, carry):
            for u in range(8):
                r = o * 8 + u
                q = j * span + r
                s = idx_s[q // cap, q % cap]
                xbuf[pl.ds(r, 1), :] = tab[pl.ds(s, 1), :]
            return carry

        lax.fori_loop(0, span // 8, fill, 0)
        x_t[:, j * span : (j + 1) * span] = xbuf[...].T.astype(BF16)
        if j == total // span // 2:
            forward(0)
    forward(1)
    for layer in range(2):
        wa = wholes[layer]
        part = wa.at[p2, pl.ds(half * (1 - dx), half)]
        onward[layer].wait_recv()
        late[layer] = remote(
            part, part, ag_send.at[layer, 4], ag_recv.at[layer, 4], (d, p1)
        )
        late[layer].start()
    for layer in range(2):
        own[layer].wait()
        core[layer].wait()
        across[layer].wait_send()
        onward[layer].wait_send()
        spread[layer].wait()
        late[layer].wait()


def fetch(n_dp, cap, owner, slot, cot, ws1, ws2, table):
    rows, width = owner.shape[1], table.shape[1]
    total = n_dp * cap
    step = min(1024, table.shape[0])
    whole = (4,) + ws1.shape
    dma = pltpu.SemaphoreType.DMA
    vmem = pl.BlockSpec(memory_space=VMEM)
    hbm = pl.BlockSpec(memory_space=ANY)
    return pl.pallas_call(
        functools.partial(fetch_kernel, n_dp, cap),
        out_shape=[
            jax.ShapeDtypeStruct((width, total), BF16),
            jax.ShapeDtypeStruct((n_dp, 8, cap), F32),
            jax.ShapeDtypeStruct((1, rows), jnp.int32),
            jax.ShapeDtypeStruct(whole, BF16),
            jax.ShapeDtypeStruct(whole, BF16),
        ],
        in_specs=[vmem] * 3 + [hbm] * 3,
        out_specs=[vmem] * 3 + [hbm] * 2,
        scratch_shapes=[
            pltpu.VMEM((n_dp, 8, cap), F32),
            pltpu.VMEM((n_dp, 8, cap), F32),
            pltpu.VMEM((n_dp, cap), jnp.int32),
            pltpu.SMEM((n_dp, cap), jnp.int32),
            pltpu.VMEM((2, step, width), BF16),
            pltpu.VMEM((table.shape[0], width), F32),
            pltpu.VMEM((256, width), F32),
            dma((2,)),
            dma((2, 5)),
            dma((2, 5)),
            dma((n_dp,)),
            dma((n_dp,)),
            dma,
            dma((2,)),
        ],
        compiler_params=pltpu.CompilerParams(
            collective_id=0, has_side_effects=True, vmem_limit_bytes=50 * MIB
        ),
    )(owner, slot, cot, ws1, ws2, table)


def forward_kernel(tasks, x_t, wa, gate, bo, h, s, y, g, out, z):
    e = pl.program_id(0)
    wide = x_t.shape[1] // 128

    @pl.when(e == 0)
    def _():
        logits = dot(gate[...], x_t[...])
        for t in range(tasks):
            part = logits[8 * t : 8 * t + 8]
            top = jnp.exp(part - jnp.max(part, axis=0, keepdims=True))
            g[t] = top / jnp.sum(top, axis=0, keepdims=True)
        z[...] = jnp.zeros_like(z)

    block = wa[...].reshape(256, wa.shape[3])
    bias = block[:, 768:896].astype(F32)
    pre = dot(block[:, :512], x_t[...]) + jnp.concatenate([bias] * wide, axis=1)
    u = pre * 0.5
    th = jnp.tanh(u)
    a = 1.0 + th
    smooth = u * a
    hb = smooth.astype(BF16)
    h[0] = hb
    s[0] = (0.5 * (a + smooth * (1.0 - th))).astype(BF16)
    out_bias = bo[0].astype(F32)
    ye = dot(block[:, 512:768], hb, TN) + jnp.concatenate([out_bias] * wide, axis=1)
    y[0] = ye.astype(BF16)
    for t in range(tasks):
        z[t] += g[t, pl.ds(e, 1), :] * ye

    @pl.when(e == pl.num_programs(0) - 1)
    def _():
        for t in range(tasks):
            out[256 * t : 256 * t + 256, :] = z[t].astype(BF16)


def layer_forward(x_t, wa, gate, bo, tasks):
    total = x_t.shape[1]
    act = jax.ShapeDtypeStruct((8, 256, total), BF16)
    per = pl.BlockSpec((1, 256, total), lambda e: (e, 0, 0))
    return pl.pallas_call(
        functools.partial(forward_kernel, tasks),
        grid=(8,),
        out_shape=[
            act, act, act,
            jax.ShapeDtypeStruct((tasks, 8, total), F32),
            jax.ShapeDtypeStruct((256 * tasks, total), BF16),
        ],
        in_specs=[
            pl.BlockSpec(x_t.shape, lambda e: (0, 0)),
            pl.BlockSpec((4, 1, 64, wa.shape[3]), lambda e: (0, e, 0, 0)),
            pl.BlockSpec(gate.shape, lambda e: (0, 0)),
            pl.BlockSpec((1, 256, 128), lambda e: (e, 0, 0)),
        ],
        out_specs=[
            per, per, per,
            pl.BlockSpec((tasks, 8, total), lambda e: (0, 0, 0)),
            pl.BlockSpec((256 * tasks, total), lambda e: (0, 0)),
        ],
        scratch_shapes=[pltpu.VMEM((tasks, 256, total), F32)],
        compiler_params=pltpu.CompilerParams(vmem_limit_bytes=58 * MIB),
    )(x_t, wa, gate, bo)


def tower_kernel(zb, w, vec, cot, pred, dz, dw, sums):
    t = pl.program_id(0)
    wide = zb.shape[1] // 128

    def spread(v):
        return jnp.concatenate([v.astype(F32)] * wide, axis=1)

    zt, wt = zb[...], w[0]
    act = dot(wt, zt, TN) + spread(vec[0, 0])
    out_w = spread(vec[0, 1])
    sig = 0.5 + 0.5 * jnp.tanh(0.5 * act)
    smooth = act * sig
    logit = jnp.sum(smooth * out_w, axis=0, keepdims=True) + spread(vec[0, 2, 0:1])
    prob = jax.nn.sigmoid(logit)
    pred[pl.ds(t, 1), :] = prob
    dlogit = cot[pl.ds(t + 1, 1), :] * prob * (1.0 - prob)
    dact = dlogit * out_w * (sig + smooth * (1.0 - sig))
    dab = dact.astype(BF16)
    dz[...] = dot(wt, dab).astype(BF16)
    dw[...] = dot(dab, zt, NT)
    lane = lax.broadcasted_iota(jnp.int32, (128, 128), 1)
    one = jnp.sum(dact, axis=1, keepdims=True)
    two = jnp.sum(dlogit * smooth, axis=1, keepdims=True)
    three = jnp.sum(dlogit, axis=1, keepdims=True)
    sums[0] = jnp.where(lane == 0, one, jnp.where(lane == 1, two, three))


def towers(zb, w, vec, cot):
    total = zb.shape[1]
    return pl.pallas_call(
        tower_kernel,
        grid=(3,),
        out_shape=[
            jax.ShapeDtypeStruct((8, total), F32),
            jax.ShapeDtypeStruct((768, total), BF16),
            jax.ShapeDtypeStruct((128, 768), F32),
            jax.ShapeDtypeStruct((3, 128, 128), F32),
        ],
        in_specs=[
            pl.BlockSpec((256, total), lambda t: (t, 0)),
            pl.BlockSpec((1, 256, 128), lambda t: (t, 0, 0)),
            pl.BlockSpec((1, 3, 128, 128), lambda t: (t, 0, 0, 0)),
            pl.BlockSpec((8, total), lambda t: (0, 0)),
        ],
        out_specs=[
            pl.BlockSpec((8, total), lambda t: (0, 0)),
            pl.BlockSpec((256, total), lambda t: (t, 0)),
            pl.BlockSpec((128, 256), lambda t: (0, t)),
            pl.BlockSpec((1, 128, 128), lambda t: (t, 0, 0)),
        ],
        compiler_params=pltpu.CompilerParams(vmem_limit_bytes=58 * MIB),
    )(zb, w, vec, cot)


def backward_kernel(tasks, by_rows, x_t, wa, gate, g, dz, h, s, y, grads, dx, dgate, sums, acc, dg):
    e = pl.program_id(0)

    @pl.when(e == 0)
    def _():
        acc[...] = jnp.zeros_like(acc)
        sums[...] = jnp.zeros_like(sums)

    block = wa[...].reshape(256, wa.shape[3])
    ye = y[0].astype(F32)
    dy = None
    for t in range(tasks):
        dzt = dz[256 * t : 256 * t + 256, :].astype(F32)
        term = g[t, pl.ds(e, 1), :] * dzt
        dy = term if dy is None else dy + term
        dg[t, pl.ds(e, 1), :] = jnp.sum(dzt * ye, axis=0, keepdims=True)
    dyb = dy.astype(BF16)
    dpre = dot(block[:, 512:768], dyb) * s[0].astype(F32)
    dpb = dpre.astype(BF16)
    grads[0, :, 0:512] = dot(dpb, x_t[...], NT).astype(BF16)
    grads[0, :, 512:768] = dot(h[0], dyb, NT).astype(BF16)
    acc[...] += dot(block[:, :512], dpb, TN)
    lane = lax.broadcasted_iota(jnp.int32, (256, 128), 1)
    one = jnp.sum(dy, axis=1, keepdims=True)
    two = jnp.sum(dpre, axis=1, keepdims=True)
    sums[...] += jnp.where(lane == e, one, jnp.where(lane == e + 8, two, 0.0))

    @pl.when(e == pl.num_programs(0) - 1)
    def _():
        parts = []
        for t in range(tasks):
            gt, dgt = g[t], dg[t]
            parts.append(gt * (dgt - jnp.sum(gt * dgt, axis=0, keepdims=True)))
        dlogits = jnp.concatenate(parts, axis=0).astype(BF16)
        dgate[...] = dot(dlogits, x_t[...], NT)
        whole = acc[...] + dot(gate[...], dlogits, TN)
        if by_rows:
            for q in range(4):
                dx[q] = whole[128 * q : 128 * q + 128, :].T.astype(BF16)
        else:
            dx[...] = whole.astype(BF16)


def layer_backward(x_t, wa, gate, g, dz, h, s, y, tasks, by_rows):
    total = x_t.shape[1]
    per = pl.BlockSpec((1, 256, total), lambda e: (e, 0, 0))
    dx = (4, total, 128) if by_rows else (512, total)
    return pl.pallas_call(
        functools.partial(backward_kernel, tasks, by_rows),
        grid=(8,),
        out_shape=[
            jax.ShapeDtypeStruct((8, 256, 768), BF16),
            jax.ShapeDtypeStruct(dx, BF16),
            jax.ShapeDtypeStruct(gate.shape, F32),
            jax.ShapeDtypeStruct((256, 128), F32),
        ],
        in_specs=[
            pl.BlockSpec(x_t.shape, lambda e: (0, 0)),
            pl.BlockSpec((4, 1, 64, wa.shape[3]), lambda e: (0, e, 0, 0)),
            pl.BlockSpec(gate.shape, lambda e: (0, 0)),
            pl.BlockSpec(g.shape, lambda e: (0, 0, 0)),
            pl.BlockSpec(dz.shape, lambda e: (0, 0)),
            per, per, per,
        ],
        out_specs=[
            pl.BlockSpec((1, 256, 768), lambda e: (e, 0, 0)),
            pl.BlockSpec(dx, lambda e: (0,) * len(dx)),
            pl.BlockSpec(gate.shape, lambda e: (0, 0)),
            pl.BlockSpec((256, 128), lambda e: (0, 0)),
        ],
        scratch_shapes=[
            pltpu.VMEM((512, total), F32),
            pltpu.VMEM((tasks, 8, total), F32),
        ],
        compiler_params=pltpu.CompilerParams(vmem_limit_bytes=58 * MIB),
    )(x_t, wa, gate, g, dz, h, s, y)


UNITS = 9


def sum_kernel(
    n_dp, grads, dxq, req, pred, place,
    shard, shared, dx_all, req_all, pred_out,
    core_in, mine, y_in, half, x_in, quarter, z_in, piece, gathered, pred_send, pred_recv,
    sem_s, sem_r, z_send, z_recv, zz_send, zz_recv, dx_send, dx_recv, rq_send, rq_recv, p_send, p_recv, loc,
):
    d, p, p1, p2, d1 = partners(n_dp)
    deep = n_dp // 2
    full = deep == 4
    z, dx, py, pc = d // 2, d % 2, p // 2, p % 2
    cap = pred_send.shape[2]
    greet([((d + k) % n_dp, p) for k in range(1, n_dp)] + [(d, (p + k) % 4) for k in range(1, 4)])

    back = []
    for i in range(n_dp):
        pred_send[i] = pred[i]
    for k in range(1, n_dp):
        to = (d + k) % n_dp
        back.append(remote(pred_send.at[to], pred_recv.at[d], p_send.at[k], p_recv.at[k], (to, p)))
        back[-1].start()
    pred_recv[d] = pred_send[d]

    moves = []
    for k in range(1, 4):
        to = (p + k) % 4
        moves.append(remote(dxq.at[to], dx_all.at[p], dx_send.at[k], dx_recv.at[k], (d, to)))
        moves.append(remote(req, req_all.at[p], rq_send.at[k], rq_recv.at[k], (d, to)))
    keep = [
        pltpu.make_async_copy(dxq.at[p], dx_all.at[p], loc.at[0]),
        pltpu.make_async_copy(req, req_all.at[p], loc.at[1]),
    ]

    started = {}

    def go(name, copy):
        copy.start()
        started.setdefault(name, []).append(copy)

    def stage0(u):
        for yy in range(2):
            go((0, u), remote(
                grads.at[u, :, 2 * yy + (1 - pc)], core_in.at[u, yy],
                sem_s.at[u, yy], sem_r.at[u, yy], (d, p1)))

    def stage1(u):
        for copy in started[(0, u)]:
            copy.wait()
        for yy in range(2):
            mine[u, yy] = (
                grads[u, :, 2 * yy + pc].astype(F32) + core_in[u, yy].astype(F32)
            ).astype(BF16)
        go((1, u), remote(
            mine.at[u, 1 - py], y_in.at[u], sem_s.at[u, 2], sem_r.at[u, 2], (d, p2)))

    def stage2(u):
        for copy in started[(1, u)]:
            copy.wait()
        total = mine[u, py].astype(F32) + y_in[u].astype(F32)
        if not full:
            shard[u] = total
            return
        for xh in range(2):
            half[u, xh] = total[:, xh].astype(BF16)
        go((2, u), remote(
            half.at[u, 1 - dx], x_in.at[u], sem_s.at[u, 3], sem_r.at[u, 3], (d1, p)))

    def stage3(u):
        for copy in started[(2, u)]:
            copy.wait()
        quarter[u] = (half[u, dx].astype(F32) + x_in[u].astype(F32)).astype(BF16)
        for k in range(1, 4):
            to = (z + k) % 4
            go((3, u), remote(
                quarter.at[u, to // 2, to % 2], z_in.at[u, k],
                z_send.at[u, k], z_recv.at[u, k], (2 * to + dx, p)))

    def stage4(u):
        for copy in started[(3, u)]:
            copy.wait()
        total = quarter[u, z // 2, z % 2].astype(F32)
        for k in range(1, 4):
            total = total + z_in[u, k].astype(F32)
        piece[u] = total.astype(BF16)
        gathered[u, dx, z] = piece[u]
        for k in range(1, 4):
            to = (z + k) % 4
            go((4, u), remote(
                piece.at[u], gathered.at[u, dx, z],
                zz_send.at[u, k], zz_recv.at[u, k], (2 * to + dx, p)))

    def stage5(u):
        for copy in started[(4, u)]:
            copy.wait()
        go((5, u), remote(
            gathered.at[u, dx], gathered.at[u, dx], sem_s.at[u, 4], sem_r.at[u, 4], (d1, p)))

    def stage6(u):
        for copy in started[(5, u)]:
            copy.wait()
        for xh in range(2):
            for e in range(2):
                for zr in range(2):
                    shard[u, e, xh, zr] = gathered[u, xh, 2 * e + zr].astype(F32)

    stages = [stage0, stage1, stage2] + ([stage3, stage4, stage5, stage6] if full else [])
    for tick in range(UNITS + len(stages) - 1):
        for at in range(len(stages) - 1, -1, -1):
            u = tick - at
            if 0 <= u < UNITS:
                stages[at](u)
        if tick == 1:
            for move in moves + keep:
                move.start()
    last = UNITS - 1
    if full:
        shared[p] = gathered[last]
        again = [
            remote(gathered.at[last], shared.at[p], sem_s.at[k, 5], sem_r.at[k, 5], (d, (p + k) % 4))
            for k in range(1, 4)
        ]
        for copy in again:
            copy.start()
    else:
        again = []
    for copy in back:
        copy.wait()
    rows = place.shape[1]
    out = jnp.zeros((16, rows), F32)
    for i in range(n_dp):
        c = pred_recv[i]
        high = c.astype(BF16).astype(F32)
        low = c - high
        both = jnp.concatenate([high, low], axis=0).astype(BF16)
        at = lax.broadcasted_iota(jnp.int32, (cap, rows), 0) + i * cap
        pick = jnp.where(at == place[...], 1.0, 0.0).astype(BF16)
        out = out + dot(both, pick)
    pred_out[...] = (out[0:8] + out[8:16])[0:3]
    for copy in again:
        copy.wait()
    for move in moves + keep:
        move.wait()


def sum_up(n_dp, grads, dxq, req, pred, place):
    full = n_dp == 8
    cap = pred.shape[2]
    rows = place.shape[1]
    dma = pltpu.SemaphoreType.DMA
    vmem = pl.BlockSpec(memory_space=VMEM)
    hbm = pl.BlockSpec(memory_space=ANY)
    part = (2, 2, 16, 768)
    return pl.pallas_call(
        functools.partial(sum_kernel, n_dp),
        out_shape=[
            jax.ShapeDtypeStruct((UNITS, 2) + part, F32),
            jax.ShapeDtypeStruct((4, 2, 4, 16, 768), BF16),
            jax.ShapeDtypeStruct(dxq.shape, BF16),
            jax.ShapeDtypeStruct((4,) + req.shape, F32),
            jax.ShapeDtypeStruct((3, rows), F32),
        ],
        in_specs=[vmem, hbm, hbm, vmem, vmem],
        out_specs=[vmem, vmem, hbm, hbm, vmem],
        scratch_shapes=[
            pltpu.VMEM((UNITS, 2, 2) + part, BF16),
            pltpu.VMEM((UNITS, 2, 2) + part, BF16),
            pltpu.VMEM((UNITS, 2) + part, BF16),
            pltpu.VMEM((UNITS, 2, 2, 2, 16, 768), BF16),
            pltpu.VMEM((UNITS, 2, 2, 16, 768), BF16),
            pltpu.VMEM((UNITS, 2, 2, 16, 768), BF16),
            pltpu.VMEM((UNITS, 4, 16, 768), BF16),
            pltpu.VMEM((UNITS, 16, 768), BF16),
            pltpu.VMEM((UNITS, 2, 4, 16, 768), BF16),
            pltpu.VMEM((n_dp, 8, cap), F32),
            pltpu.VMEM((n_dp, 8, cap), F32),
            dma((UNITS, 6)),
            dma((UNITS, 6)),
            dma((UNITS, 4)),
            dma((UNITS, 4)),
            dma((UNITS, 4)),
            dma((UNITS, 4)),
            dma((4,)),
            dma((4,)),
            dma((4,)),
            dma((4,)),
            dma((n_dp,)),
            dma((n_dp,)),
            dma((2,)),
        ],
        compiler_params=pltpu.CompilerParams(
            collective_id=1, has_side_effects=True, vmem_limit_bytes=58 * MIB
        ),
    )(grads, dxq, req, pred, place)


def scatter_kernel(slots, dx, out, a0, a1, a2, a3, buf):
    parts = (a0, a1, a2, a3)
    span = buf.shape[1]
    for a in parts:
        a[...] = jnp.zeros_like(a)

    def block(j, carry):
        at = pl.multiple_of(j * span, span)
        for q in range(4):
            buf[q] = dx[q, pl.ds(at, span), :].astype(F32)

        def add(o, inner):
            for u in range(4):
                r = o * 4 + u
                for q in range(4):
                    to = pl.ds(slots[q, at + r], 1)
                    parts[q][to, :] += buf[q, pl.ds(r, 1), :]
            return inner

        lax.fori_loop(0, span // 4, add, 0)
        return carry

    lax.fori_loop(0, dx.shape[1] // span, block, 0)
    out[...] = (a0[...] + a1[...]) + (a2[...] + a3[...])


def scatter(slots, dx, rows):
    vmem = pl.BlockSpec(memory_space=VMEM)
    table = (rows, 128)
    return pl.pallas_call(
        scatter_kernel,
        out_shape=jax.ShapeDtypeStruct(table, F32),
        in_specs=[pl.BlockSpec(memory_space=pltpu.SMEM), vmem],
        out_specs=vmem,
        scratch_shapes=[pltpu.VMEM(table, F32)] * 4 + [pltpu.VMEM((4, 256, 128), F32)],
        compiler_params=pltpu.CompilerParams(vmem_limit_bytes=58 * MIB),
    )(slots, dx)


def shard_of(w_in, b_in, w_out):
    bias = jnp.broadcast_to(b_in[:, :, None], b_in.shape + (128,))
    return jnp.concatenate([w_in.transpose(1, 2, 0), w_out, bias], axis=2)


def on_device(
    owner, slot, table, w_in1, b_in1, w_out1, b_out1, gate1,
    w_in2, b_in2, w_out2, b_out2, gate2,
    tower_in, tower_bias, tower_out, tower_out_bias, pred_cot,
):
    n_dp = lax.axis_size("dp")
    rows = owner.shape[0]
    cap = 4 * rows // n_dp
    total = n_dp * cap
    x1, req, place, wa1, wa2 = fetch(
        n_dp,
        cap,
        owner.reshape(1, rows),
        slot.reshape(1, rows),
        pred_cot,
        shard_of(w_in1, b_in1, w_out1),
        shard_of(w_in2, b_in2, w_out2),
        table,
    )
    flat = req.transpose(1, 0, 2).reshape(8, total)
    bo1 = jnp.broadcast_to(b_out1[:, :, None], b_out1.shape + (128,))
    bo2 = jnp.broadcast_to(b_out2[:, :, None], b_out2.shape + (128,))
    g1t = gate1.reshape(gate1.shape[0], -1).T
    g2t = gate2.reshape(gate2.shape[0], -1).T
    vec = jnp.stack(
        [
            tower_bias,
            tower_out,
            jnp.broadcast_to(tower_out_bias[:, None], tower_out.shape),
        ],
        axis=1,
    )
    vec = jnp.broadcast_to(vec[:, :, :, None], vec.shape + (128,))
    h1, s1, y1, g1, x2 = layer_forward(x1, wa1, g1t, bo1, 2)
    h2, s2, y2, g2, zb = layer_forward(x2, wa2, g2t, bo2, 3)
    pred, dz2, dtower, tsums = towers(zb, tower_in, vec, flat)
    grads2, dz1, dgate2, sums2 = layer_backward(x2, wa2, g2t, g2, dz2, h2, s2, y2, 3, False)
    grads1, dxq, dgate1, sums1 = layer_backward(x1, wa1, g1t, g1, dz1, h1, s1, y1, 2, True)
    biases = jnp.concatenate([sums1[:, :16], sums2[:, :16]], axis=1).T
    gates = jnp.concatenate([dgate1, dgate2], axis=0)
    small = tsums[:, :, :3].transpose(2, 0, 1).reshape(3, 384)
    small = jnp.concatenate([small.reshape(1, -1), jnp.zeros((1, 768 * 2 - 1152), F32)], axis=1)
    small = small.reshape(2, 768)
    shared = jnp.concatenate(
        [
            dtower,
            jnp.concatenate([gates, jnp.pad(biases, ((0, 8), (0, 0)))], axis=1),
            small,
            jnp.zeros((512 - 128 - 40 - 2, 768), F32),
        ],
        axis=0,
    ).astype(BF16)
    grads = jnp.concatenate([grads2, grads1, shared.reshape(2, 256, 768)], axis=0)
    grads = grads.reshape(UNITS, 2, 4, 2, 2, 16, 768)
    by_source = pred.reshape(8, n_dp, cap).transpose(1, 0, 2)
    sums, whole, dx_all, req_all, predictions = sum_up(n_dp, grads, dxq, req, by_source, place)
    if n_dp == 8:
        whole = whole.reshape(4, 2, 2, 2, 16, 768).transpose(2, 0, 1, 3, 4, 5)
        whole = whole.reshape(512, 768).astype(F32)
    else:
        sums = lax.psum(sums, "dp")
        whole = lax.all_gather(sums[UNITS - 1], "mp", axis=0)
        whole = whole.transpose(1, 0, 2, 3, 4, 5).reshape(512, 768)
    sums = sums[: UNITS - 1].reshape(2, 8, 64, 768)
    slots = req_all[:, :, 0, :].reshape(4, total).astype(jnp.int32)
    table_grad = scatter(slots, dx_all, table.shape[0])
    dtower, gates, biases = whole[:128], whole[128:168, :512], whole[128:160, 512:]
    small = whole[168:170].reshape(-1)[:1152].reshape(3, 3, 128)
    inner = w_in1.shape[2]
    start = lax.axis_index("mp") * inner
    b_in = [lax.dynamic_slice_in_dim(biases[k : k + 8], start, inner, axis=1) for k in (8, 24)]
    w_in = [sums[k, :, :, :512].transpose(2, 0, 1) for k in (1, 0)]
    return (
        predictions,
        table_grad,
        w_in[0],
        b_in[0],
        sums[1, :, :, 512:],
        biases[0:8],
        gates[:16].T.reshape(gate1.shape),
        w_in[1],
        b_in[1],
        sums[0, :, :, 512:],
        biases[16:24],
        gates[16:40].T.reshape(gate2.shape),
        dtower.reshape(128, 3, 256).transpose(1, 2, 0),
        small[0],
        small[1],
        small[2, :, 0],
    )


def solution(mesh):
    in_specs = (
        P(("dp", "mp"), None),
        P(("dp", "mp")),
        P("dp", None),
        P(None, None, "mp"),
        P(None, "mp"),
        P(None, "mp", None),
        P(),
        P(),
        P(None, None, "mp"),
        P(None, "mp"),
        P(None, "mp", None),
        P(),
        P(),
        P(),
        P(),
        P(),
        P(),
        P(None, ("dp", "mp")),
    )
    out_specs = (
        P(None, ("dp", "mp")),
        P("dp", "mp"),
        P(None, None, "mp"),
        P(None, "mp"),
        P(None, "mp", None),
        P(),
        P(),
        P(None, None, "mp"),
        P(None, "mp"),
        P(None, "mp", None),
        P(),
        P(),
        P(),
        P(),
        P(),
        P(),
    )
    return jax.shard_map(
        on_device, mesh=mesh, in_specs=in_specs, out_specs=out_specs, check_vma=False
    )
```

time: 889 us -> 325 us (0.37)
  waiting for transfers between devices: 652 us -> 0 us
  Pallas kernels: 0 us -> 283 us
  matrix products: 64.1 us -> 0 us
  local copies, waits for them, and re-layouts: 65 us -> 28.6 us
  blocking collectives: 31.1 us -> 0 us
  other arithmetic: 39.9 us -> 10.8 us
  starting transfers between devices: 16.8 us -> 0 us
  between operations: 14.9 us -> 0.9 us
    psum x3 -> x0, waiting for transfers between devices: 381 us -> none  [the longest x2 247 us: on_device(): lax.psum((shared_one[0], shared_one[1], shared_two[0], shared_two[1], tow...]
    pallas_call x0 -> x8, Pallas kernels: none -> 283 us  [the longest x1 111 us: sum_up(): pl.pallas_call(functools.partial(sum_kernel, n_dp), out_shape=[jax.ShapeD...]
    reduce_scatter x5 -> x0, waiting for transfers between devices: 210 us -> none  [the longest x1 128 us: on_device(): lax.psum_scatter(table_part, 'mp', scatter_dimension=1, tiled=True)]
    dot_general x24 -> x0, matrix products: 56.9 us -> none  [the longest x2 11.9 us: layer_forward(): jnp.dot(inputs, w_in.reshape(width, -1), preferred_element_type=jnp.float32)]
    all_to_all x3 -> x0, waiting for transfers between devices: 37.9 us -> none  [the longest x1 30.7 us: on_device(): lax.all_to_all(served, 'dp', split_axis=0, concat_axis=0, tiled=True)]
    unnamed x16 -> x0, waiting for transfers between devices: 22.3 us -> none
    scatter-add x1 -> x0, other arithmetic: 21.7 us -> none  [on_device(): jnp.zeros((table.shape[0], width), jnp.float32).at[wanted].add(arrived)]
    psum x1 -> x0, blocking collectives: 18.4 us -> none  [on_device(): lax.psum((sharded[0], sharded[1], sharded[2], sharded[3], sharded[4], sha...]
  transfers between devices with their start and end apart: 17 -> 0, of which waited for: 10 -> 0; matrix products, arithmetic and copies ran while one was open for 16% -> 0% of each run, Pallas kernels for 0% -> 0%
where the time goes in v1:
time: 325 us; the launch traced here: 324 us
  Pallas kernels  283 us (87%)
  local copies, waits for them, and re-layouts  28.6 us (9%)
  other arithmetic  10.8 us (3%)
    pallas_call x1, Pallas kernels, sum_up(): pl.pallas_call(functools.partial(sum_kernel, n_dp), out_shape=[jax.ShapeD...  111 us
    pallas_call x2, Pallas kernels, layer_backward(): pl.pallas_call(functools.partial(backward_kernel, tasks, by_rows), grid=(...  53.6 us
    pallas_call x1, Pallas kernels, fetch(): pl.pallas_call(functools.partial(fetch_kernel, n_dp, cap), out_shape=[jax...  50.7 us
    pallas_call x2, Pallas kernels, layer_forward(): pl.pallas_call(functools.partial(forward_kernel, tasks), grid=(8,), out_s...  40.4 us
    pallas_call x1, Pallas kernels, scatter(): pl.pallas_call(scatter_kernel, out_shape=jax.ShapeDtypeStruct(table, F32)...  21.4 us
    pallas_call x1, Pallas kernels, towers(): pl.pallas_call(tower_kernel, grid=(3,), out_shape=[jax.ShapeDtypeStruct((...  6.6 us

profile of v1, /device:TPU:1, one launch (start us, length us, event | category | flops | bytes accessed | tf_op | source)
XLA Modules:
  0.0 323.7 jit_solution(4389118693903920579)
XLA Ops:
  2.3 1.6 pad_maximum_fusion.1
  4.0 50.7 %shard_map.297 = (bf16[512,2048]{1,0:T(8,128)(2,1)S(1)}, f32[8,8,256]{2,1,0:T(8,128)S(1)}, s32[1,512]{1,0:T(1,128)S(1)}, bf16[4,8,64,896]{3,2,1,0:T(8,128)(2,1)}, bf16[4,8,64,896]{3,2,1,0:T(8,128)(2,1)}) custom-call(s32[1,512]{1,0:T(1,128)S(1)} %bitcast.56, s32[1,512]{1,0:T(1,128)S(1)} %bitcast.57, f32[3,512]{1,0:T(4,128)S(1)} %copy-done.2, ...), custom_call_target="tpu_custom_call" | custom-call | tf_op jit(solution)/shard_map/pallas_call | solution.py:215
  54.7 1.3 copy-done
  57.2 1.1 broadcast_in_dim.14.bo
  58.3 19.1 %shard_map.298 = (bf16[8,256,2048]{2,1,0:T(8,128)(2,1)}, bf16[8,256,2048]{2,1,0:T(8,128)(2,1)}, bf16[8,256,2048]{2,1,0:T(8,128)(2,1)}, f32[2,8,2048]{2,1,0:T(8,128)}, bf16[512,2048]{1,0:T(8,128)(2,1)}) custom-call(bf16[512,2048]{1,0:T(8,128)(2,1)} %copy-done, bf16[4,8,64,896]{3,2,1,0:T(8,128)(2,1)} %get-tuple-element.49.wa, bf16[16,512]{1,0:T(8,128)(2,1)} %bitcast.75, ...), custom_call_target="tpu_custom_call" | custom-call | tf_op jit(solution)/shard_map/pallas_call | solution.py:287
  77.4 1.1 broadcast_in_dim.15.bo
  78.6 21.3 %shard_map.299 = (bf16[8,256,2048]{2,1,0:T(8,128)(2,1)}, bf16[8,256,2048]{2,1,0:T(8,128)(2,1)}, bf16[8,256,2048]{2,1,0:T(8,128)(2,1)}, f32[3,8,2048]{2,1,0:T(8,128)}, bf16[768,2048]{1,0:T(8,128)(2,1)}) custom-call(bf16[512,2048]{1,0:T(8,128)(2,1)} %get-tuple-element.50.x_t, bf16[4,8,64,896]{3,2,1,0:T(8,128)(2,1)} %get-tuple-element.51.wa, ...), custom_call_target="tpu_custom_call" | custom-call | tf_op jit(solution)/shard_map/pallas_call | solution.py:287
  99.9 0.9 broadcast_in_dim.16.vec
  100.9 6.6 %shard_map.300 = (f32[8,2048]{1,0:T(8,128)}, bf16[768,2048]{1,0:T(8,128)(2,1)}, f32[128,768]{1,0:T(8,128)}, f32[3,128,128]{2,1,0:T(8,128)}) custom-call(bf16[768,2048]{1,0:T(8,128)(2,1)} %get-tuple-element.53.zb, bf16[3,256,128]{2,1,0:T(8,128)(2,1)} %w.1, bf16[3,3,128,128]{3,2,1,0:T(8,128)(2,1)} %broadcast_in_dim.16.vec, f32[8,2048]{1,0:T(8,128)} %bitcast.55), custom_call_target="tpu_custom_call" | custom-call | tf_op jit(solution)/shard_map/pallas_call | solution.py:340
  107.5 0.9 fusion.8
  109.2 28.1 %shard_map.301 = (bf16[8,256,768]{2,1,0:T(8,128)(2,1)}, bf16[512,2048]{1,0:T(8,128)(2,1)}, f32[24,512]{1,0:T(8,128)}, f32[256,128]{1,0:T(8,128)}) custom-call(bf16[512,2048]{1,0:T(8,128)(2,1)} %get-tuple-element.50.x_t, bf16[4,8,64,896]{3,2,1,0:T(8,128)(2,1)} %get-tuple-element.51.wa, bf16[24,512]{1,0:T(8,128)(2,1)} %bitcast.74, ...), custom_call_target="tpu_custom_call" | custom-call | tf_op jit(solution)/shard_map/pallas_call | solution.py:412
  138.3 25.4 %shard_map.302 = (bf16[8,256,768]{2,1,0:T(8,128)(2,1)}, bf16[4,2048,128]{2,1,0:T(8,128)(2,1)}, f32[16,512]{1,0:T(8,128)}, f32[256,128]{1,0:T(8,128)}) custom-call(bf16[512,2048]{1,0:T(8,128)(2,1)} %copy-done, bf16[4,8,64,896]{3,2,1,0:T(8,128)(2,1)} %get-tuple-element.49.wa, bf16[16,512]{1,0:T(8,128)(2,1)} %bitcast.76, f32[2,8,2048]{2,1,0:T(8,128)} %get-tuple-element.60.g, ...), custom_call_target="tpu_custom_call" | custom-call | tf_op jit(solution)/shard_map/pallas_call | solution.py:412
  163.8 1.5 slice.140
  168.8 5.5 %pad_maximum_fusion = bf16[18,256,768]{2,1,0:T(8,128)(2,1)} fusion(bf16[2,256,768]{2,1,0:T(8,128)(2,1)S(1)} %bitcast.61, bf16[8,256,768]{2,1,0:T(8,128)(2,1)} %get-tuple-element.65, bf16[8,256,768]{2,1,0:T(8,128)(2,1)S(1)} %copy-done.6), kind=kLoop, calls=%fused_computation | loop fusion | flops 7077888 | bytes 14155776 | tf_op jit(solution)/shard_map/concatenate | solution.py:736
  174.3 110.7 %shard_map.303 = (f32[9,2,2,2,16,768]{5,4,3,2,1,0:T(8,128)}, bf16[4,2,4,16,768]{4,3,2,1,0:T(8,128)(2,1)}, bf16[4,2048,128]{2,1,0:T(8,128)(2,1)}, f32[4,8,8,256]{3,2,1,0:T(8,128)}, f32[3,512]{1,0:T(4,128)}) custom-call(bf16[9,2,4,2,2,16,768]{6,5,4,3,2,1,0:T(8,128)(2,1)} %bitcast.58, bf16[4,2048,128]{2,1,0:T(8,128)(2,1)} %get-tuple-element.72.dxq, ...), custom_call_target="tpu_custom_call" | custom-call | tf_op jit(solution)/shard_map/pallas_call | solution.py:597
  285.1 1.0 convert_reduce_fusion
  286.7 21.4 %shard_map.304 = f32[8192,128]{1,0:T(8,128)} custom-call(s32[4,2048]{1,0:T(4,128)} %bitcast.71, bf16[4,2048,128]{2,1,0:T(8,128)(2,1)} %get-tuple-element.77.dx), custom_call_target="tpu_custom_call" | custom-call | tf_op jit(solution)/shard_map/pallas_call | solution.py:669
  308.1 2.1 slice.90
  310.3 1.6 slice_bitcast_fusion
  312.2 1.2 copy-done.7
  314.6 1.1 slice_bitcast_fusion.2
  315.7 1.4 slice_bitcast_fusion.5
  317.7 1.4 slice_bitcast_fusion.4
  319.2 1.0 slice.121
  (62 shorter events, 14.5 us)
Async XLA Ops:
  2.3 1.7 copy-start.2
  2.3 1.7 copy-start.4
  2.3 1.7 copy-start.5
  4.0 53.2 %copy-start.11 = (bf16[8,256]{1,0:T(8,128)(2,1)S(1)}, bf16[8,256]{1,0:T(8,128)(2,1)}, u32[]{:S(2)}) copy-start(bf16[8,256]{1,0:T(8,128)(2,1)} %param.24) | copy-start | bytes 12292
  54.7 1.3 copy-start
  56.0 0.6 copy-start.1
  56.6 0.6 copy-start.3
  58.3 19.1 %copy-start.12 = (bf16[8,256]{1,0:T(8,128)(2,1)S(1)}, bf16[8,256]{1,0:T(8,128)(2,1)}, u32[]{:S(2)}) copy-start(bf16[8,256]{1,0:T(8,128)(2,1)} %param.29) | copy-start | bytes 12292
  78.6 21.3 %copy-start.15 = (bf16[3]{0:T(256)(128)(2,1)S(1)}, bf16[3]{0:T(256)(128)(2,1)}, u32[]{:S(2)}) copy-start(bf16[3]{0:T(256)(128)(2,1)} %param.34) | copy-start | bytes 22
  78.6 21.4 %copy-start.13 = (bf16[3,128]{1,0:T(4,128)(2,1)S(1)}, bf16[3,128]{1,0:T(4,128)(2,1)}, u32[]{:S(2)}) copy-start(bf16[3,128]{1,0:T(4,128)(2,1)} %param.33) | copy-start | bytes 2308
  78.6 21.4 %copy-start.14 = (bf16[3,128]{1,0:T(4,128)(2,1)S(1)}, bf16[3,128]{1,0:T(4,128)(2,1)}, u32[]{:S(2)}) copy-start(bf16[3,128]{1,0:T(4,128)(2,1)} %param.32) | copy-start | bytes 2308
  138.3 29.5 %copy-start.9 = (f32[128,768]{1,0:T(8,128)S(1)}, f32[128,768]{1,0:T(8,128)}, u32[]{:S(2)}) copy-start(f32[128,768]{1,0:T(8,128)} %get-tuple-element.66) | copy-start | bytes 1179652
  138.3 30.4 %copy-start.6 = (bf16[8,256,768]{2,1,0:T(8,128)(2,1)S(1)}, bf16[8,256,768]{2,1,0:T(8,128)(2,1)}, u32[]{:S(2)}) copy-start(bf16[8,256,768]{2,1,0:T(8,128)(2,1)} %get-tuple-element.59) | copy-start | bytes 9437188
  310.2 1.6 copy-start.8
  312.2 1.2 copy-start.7
  314.6 8.5 %copy-start.10 = (f32[3,512]{1,0:T(4,128)S(1)}, f32[3,512]{1,0:T(4,128)}, u32[]{:S(2)}) copy-start(f32[3,512]{1,0:T(4,128)} %get-tuple-element.108) | copy-start | bytes 18436

commit v2 on v1

--- a/solution.py
+++ b/solution.py
@@ -332,7 +332,8 @@
     one = jnp.sum(dact, axis=1, keepdims=True)
     two = jnp.sum(dlogit * smooth, axis=1, keepdims=True)
     three = jnp.sum(dlogit, axis=1, keepdims=True)
-    sums[0] = jnp.where(lane == 0, one, jnp.where(lane == 1, two, three))
+    table = jnp.where(lane == 0, one, jnp.where(lane == 1, two, three))
+    sums[0] = table.T[0:8]
 
 
 def towers(zb, w, vec, cot):
@@ -344,7 +345,7 @@
             jax.ShapeDtypeStruct((8, total), F32),
             jax.ShapeDtypeStruct((768, total), BF16),
             jax.ShapeDtypeStruct((128, 768), F32),
-            jax.ShapeDtypeStruct((3, 128, 128), F32),
+            jax.ShapeDtypeStruct((3, 8, 128), F32),
         ],
         in_specs=[
             pl.BlockSpec((256, total), lambda t: (t, 0)),
@@ -356,285 +357,347 @@
             pl.BlockSpec((8, total), lambda t: (0, 0)),
             pl.BlockSpec((256, total), lambda t: (t, 0)),
             pl.BlockSpec((128, 256), lambda t: (0, t)),
-            pl.BlockSpec((1, 128, 128), lambda t: (t, 0, 0)),
+            pl.BlockSpec((1, 8, 128), lambda t: (t, 0, 0)),
         ],
         compiler_params=pltpu.CompilerParams(vmem_limit_bytes=58 * MIB),
     )(zb, w, vec, cot)
 
 
-def backward_kernel(tasks, by_rows, x_t, wa, gate, g, dz, h, s, y, grads, dx, dgate, sums, acc, dg):
-    e = pl.program_id(0)
-
-    @pl.when(e == 0)
+def back_kernel(
+    n_dp, x1, x2, wa1, wa2, gate1, gate2, g1, g2, dz2, h1, s1, y1, h2, s2, y2,
+    dtower, tsums, req, pred, place,
+    summed, shared, dx_all, req_all, pred_out,
+    acc, dz1, dg, sums, dgate, dxq, *rest,
+):
+    main, small, links = rest[:10], rest[10:20], rest[20:]
+    pred_send, pred_recv = links[:2]
+    sem_s, sem_r, z_s, z_r, zz_s, zz_r, dx_s, dx_r, rq_s, rq_r, p_s, p_r, again_s, again_r, loc = links[2:]
+    step = pl.program_id(0)
+    d, p, p1, p2, d1 = partners(n_dp)
+    full = n_dp == 8
+    z, dx, py, pc = d // 2, d % 2, p // 2, p % 2
+    cap = pred_send.shape[2]
+    grads = main[0]
+    units = grads.shape[0]
+
+    def copies(stage, u):
+        bufs, i = (main, u) if u < units else (small, 0)
+        own, core_in, mine, y_in, half, x_in, quarter, z_in, piece, gathered = bufs
+        if stage == 0:
+            return [
+                remote(
+                    own.at[i, :, 2 * yy + (1 - pc)], core_in.at[i, yy],
+                    sem_s.at[u, yy], sem_r.at[u, yy], (d, p1),
+                )
+                for yy in range(2)
+            ]
+        if stage == 1:
+            return [remote(mine.at[i, 1 - py], y_in.at[i], sem_s.at[u, 2], sem_r.at[u, 2], (d, p2))]
+        if stage == 2:
+            return [remote(half.at[i, 1 - dx], x_in.at[i], sem_s.at[u, 3], sem_r.at[u, 3], (d1, p))]
+        if stage == 3:
+            return [
+                remote(
+                    quarter.at[i, (z + k) % 4 // 2, (z + k) % 4 % 2], z_in.at[i, k],
+                    z_s.at[u, k], z_r.at[u, k], (2 * ((z + k) % 4) + dx, p),
+                )
+                for k in range(1, 4)
+            ]
+        if stage == 4:
+            return [
+                remote(
+                    piece.at[i], gathered.at[i, dx, z],
+                    zz_s.at[u, k], zz_r.at[u, k], (2 * ((z + k) % 4) + dx, p),
+                )
+                for k in range(1, 4)
+            ]
+        part = gathered.at[i, dx]
+        return [remote(part, part, sem_s.at[u, 4], sem_r.at[u, 4], (d1, p))]
+
+    def advance(stage, u):
+        bufs, i = (main, u) if u < units else (small, 0)
+        own, core_in, mine, y_in, half, x_in, quarter, z_in, piece, gathered = bufs
+        if stage:
+            for copy in copies(stage - 1, u):
+                copy.wait()
+        if stage == 1:
+            for yy in range(2):
+                both = own[i, :, 2 * yy + pc].astype(F32) + core_in[i, yy].astype(F32)
+                mine[i, yy] = both.astype(BF16)
+        if stage == 2:
+            both = mine[i, py].astype(F32) + y_in[i].astype(F32)
+            for xh in range(2):
+                half[i, xh] = both[:, xh].astype(BF16)
+        if stage == 3:
+            quarter[i] = (half[i, dx].astype(F32) + x_in[i].astype(F32)).astype(BF16)
+        if stage == 4:
+            both = quarter[i, z // 2, z % 2].astype(F32)
+            for k in range(1, 4):
+                both = both + z_in[i, k].astype(F32)
+            piece[i] = both.astype(BF16)
+            gathered[i, dx, z] = piece[i]
+        if stage < last_stage:
+            for copy in copies(stage, u):
+                copy.start()
+
+    last_stage = 6 if full else 2
+
+    def tick(at, count):
+        for stage in range(last_stage, -1, -1):
+            u = at - stage
+            if 0 <= u < count:
+                advance(stage, u)
+
+    def predictions_back():
+        return [
+            remote(
+                pred_send.at[(d + k) % n_dp], pred_recv.at[d], p_s.at[k], p_r.at[k],
+                ((d + k) % n_dp, p),
+            )
+            for k in range(1, n_dp)
+        ]
+
+    def requests_over():
+        return [
+            remote(req, req_all.at[p], rq_s.at[k], rq_r.at[k], (d, (p + k) % 4))
+            for k in range(1, 4)
+        ] + [pltpu.make_async_copy(req, req_all.at[p], loc.at[1])]
+
+    def columns_over():
+        return [
+            remote(dxq.at[(p + k) % 4], dx_all.at[p], dx_s.at[k], dx_r.at[k], (d, (p + k) % 4))
+            for k in range(1, 4)
+        ] + [pltpu.make_async_copy(dxq.at[p], dx_all.at[p], loc.at[0])]
+
+    @pl.when(step == 0)
     def _():
-        acc[...] = jnp.zeros_like(acc)
+        greet(
+            [((d + k) % n_dp, p) for k in range(1, n_dp)]
+            + [(d, (p + k) % 4) for k in range(1, 4)]
+        )
+        for i in range(n_dp):
+            pred_send[i] = pred[i]
+        for copy in predictions_back() + requests_over():
+            copy.start()
+        pred_recv[d] = pred_send[d]
         sums[...] = jnp.zeros_like(sums)
 
-    block = wa[...].reshape(256, wa.shape[3])
-    ye = y[0].astype(F32)
-    dy = None
-    for t in range(tasks):
-        dzt = dz[256 * t : 256 * t + 256, :].astype(F32)
-        term = g[t, pl.ds(e, 1), :] * dzt
-        dy = term if dy is None else dy + term
-        dg[t, pl.ds(e, 1), :] = jnp.sum(dzt * ye, axis=0, keepdims=True)
-    dyb = dy.astype(BF16)
-    dpre = dot(block[:, 512:768], dyb) * s[0].astype(F32)
-    dpb = dpre.astype(BF16)
-    grads[0, :, 0:512] = dot(dpb, x_t[...], NT).astype(BF16)
-    grads[0, :, 512:768] = dot(h[0], dyb, NT).astype(BF16)
-    acc[...] += dot(block[:, :512], dpb, TN)
-    lane = lax.broadcasted_iota(jnp.int32, (256, 128), 1)
-    one = jnp.sum(dy, axis=1, keepdims=True)
-    two = jnp.sum(dpre, axis=1, keepdims=True)
-    sums[...] += jnp.where(lane == e, one, jnp.where(lane == e + 8, two, 0.0))
-
-    @pl.when(e == pl.num_programs(0) - 1)
-    def _():
+    def expert(tasks, e, lanes, x_t, wa, g, dz, h, s, y):
+        block = wa[...].reshape(256, wa.shape[3])
+        ye = y[0].astype(F32)
+        dy = None
+        for t in range(tasks):
+            dzt = dz[256 * t : 256 * t + 256, :].astype(F32)
+            term = g[t, pl.ds(e, 1), :] * dzt
+            dy = term if dy is None else dy + term
+            dg[t, pl.ds(e, 1), :] = jnp.sum(dzt * ye, axis=0, keepdims=True)
+        dyb = dy.astype(BF16)
+        dpre = dot(block[:, 512:768], dyb) * s[0].astype(F32)
+        dpb = dpre.astype(BF16)
+        split = (4, 2, 2, 16)
+        grads[step // 2, step % 2, :, :, :, :, 0:512] = (
+            dot(dpb, x_t[...], NT).astype(BF16).reshape(split + (512,))
+        )
+        grads[step // 2, step % 2, :, :, :, :, 512:768] = (
+            dot(h[0], dyb, NT).astype(BF16).reshape(split + (256,))
+        )
+        prod = dot(block[:, :512], dpb, TN)
+
+        @pl.when(e == 0)
+        def _():
+            acc[...] = prod
+
+        @pl.when(e > 0)
+        def _():
+            acc[...] += prod
+
+        lane = lax.broadcasted_iota(jnp.int32, (256, 128), 1)
+        one = jnp.sum(dy, axis=1, keepdims=True)
+        two = jnp.sum(dpre, axis=1, keepdims=True)
+        sums[...] += jnp.where(
+            lane == lanes + e, one, jnp.where(lane == lanes + 8 + e, two, 0.0)
+        )
+
+    def finish(tasks, first, x_t, gate, g):
         parts = []
         for t in range(tasks):
             gt, dgt = g[t], dg[t]
             parts.append(gt * (dgt - jnp.sum(gt * dgt, axis=0, keepdims=True)))
         dlogits = jnp.concatenate(parts, axis=0).astype(BF16)
-        dgate[...] = dot(dlogits, x_t[...], NT)
-        whole = acc[...] + dot(gate[...], dlogits, TN)
-        if by_rows:
-            for q in range(4):
-                dx[q] = whole[128 * q : 128 * q + 128, :].T.astype(BF16)
+        dgate[first : first + 8 * tasks] = dot(dlogits, x_t[...], NT)
+        return acc[...] + dot(gate[...], dlogits, TN)
+
+    @pl.when(step < 8)
+    def _():
+        expert(3, step, 16, x2, wa2, g2, dz2, h2, s2, y2)
+
+    @pl.when(step == 7)
+    def _():
+        dz1[...] = finish(3, 16, x2, gate2, g2).astype(BF16)
+
+    @pl.when(step >= 8)
+    def _():
+        expert(2, step - 8, 0, x1, wa1, g1, dz1, h1, s1, y1)
+
+    for at in range(units):
+
+        @pl.when(step == 2 * at + 1)
+        def _(at=at):
+            tick(at, units)
+
+    @pl.when(step == 2 * units - 1)
+    def _():
+        whole = finish(2, 0, x1, gate1, g1)
+        for q in range(4):
+            dxq[q] = whole[128 * q : 128 * q + 128, :].T.astype(BF16)
+        own = small[0]
+        block = (2, 2, 2, 16, 256)
+        for t in range(3):
+            tower = dtower[:, 256 * t : 256 * t + 256].astype(BF16).reshape(block)
+            own[0, t // 2, 2 * (t % 2) : 2 * (t % 2) + 2] = tower
+        gates = dgate[...]
+        tail = jnp.concatenate(
+            [
+                gates[:, :256],
+                gates[:, 256:],
+                sums[...].T[:32],
+                jnp.concatenate([tsums[0], tsums[1]], axis=1),
+                jnp.concatenate([tsums[2], jnp.zeros((8, 128), F32)], axis=1),
+            ],
+            axis=0,
+        )
+        own[0, 1, 2:4] = tail.astype(BF16).reshape(block)
+        for at in range(units, units + last_stage + 1):
+            tick(at, units + 1)
+            if at == units + 1:
+                for copy in columns_over():
+                    copy.start()
+        gathered = small[9]
+
+        def again():
+            return [
+                remote(gathered.at[0], shared.at[p], again_s.at[k], again_r.at[k], (d, (p + k) % 4))
+                for k in range(1, 4)
+            ] + [pltpu.make_async_copy(gathered.at[0], shared.at[p], loc.at[2])]
+
+        result = main[9] if full else main[2]
+        out = pltpu.make_async_copy(result, summed, loc.at[3])
+        if full:
+            for copy in again():
+                copy.start()
         else:
-            dx[...] = whole.astype(BF16)
-
-
-def layer_backward(x_t, wa, gate, g, dz, h, s, y, tasks, by_rows):
-    total = x_t.shape[1]
-    per = pl.BlockSpec((1, 256, total), lambda e: (e, 0, 0))
-    dx = (4, total, 128) if by_rows else (512, total)
+            for u in range(units):
+                result[u, 0] = main[4][u].reshape(result.shape[2:])
+            pltpu.make_async_copy(small[4].at[0], shared.at[0], loc.at[2]).start()
+        out.start()
+        for copy in predictions_back():
+            copy.wait()
+        rows = place.shape[1]
+        got = jnp.zeros((16, rows), F32)
+        for i in range(n_dp):
+            c = pred_recv[i]
+            high = c.astype(BF16).astype(F32)
+            both = jnp.concatenate([high, c - high], axis=0).astype(BF16)
+            at = lax.broadcasted_iota(jnp.int32, (cap, rows), 0) + i * cap
+            pick = jnp.where(at == place[...], 1.0, 0.0).astype(BF16)
+            got = got + dot(both, pick)
+        pred_out[...] = (got[0:8] + got[8:16])[0:3]
+        for copy in requests_over() + columns_over():
+            copy.wait()
+        if full:
+            for copy in again():
+                copy.wait()
+        else:
+            pltpu.make_async_copy(small[4].at[0], shared.at[0], loc.at[2]).wait()
+        out.wait()
+
+
+def backward(n_dp, x1, x2, wa1, wa2, gate1, gate2, g1, g2, dz2, l1, l2, dtower, tsums, req, pred, place):
+    total = x1.shape[1]
+    cap, rows = pred.shape[2], place.shape[1]
+    full = n_dp == 8
+    dma = pltpu.SemaphoreType.DMA
+    hbm = pl.BlockSpec(memory_space=ANY)
+
+    def fixed(a):
+        return pl.BlockSpec(a.shape, lambda i: (0,) * a.ndim, pipeline_mode=pl.Buffered(1))
+
+    first, second = (lambda i: jnp.maximum(i - 8, 0)), (lambda i: jnp.minimum(i, 7))
+    per1 = pl.BlockSpec((1, 256, total), lambda i: (first(i), 0, 0))
+    per2 = pl.BlockSpec((1, 256, total), lambda i: (second(i), 0, 0))
+
+    def buffers(units, lanes):
+        part = (2, 2, 2, 16, lanes)
+        shapes = [
+            (units, 2, 4) + part[1:],
+            (units, 2) + part,
+            (units, 2) + part,
+            (units,) + part,
+            (units, 2, 2, 2, 16, lanes),
+            (units, 2, 2, 16, lanes),
+            (units, 2, 2, 16, lanes),
+            (units, 4, 16, lanes),
+            (units, 16, lanes),
+            (units, 2, 4, 16, lanes),
+        ]
+        return [pltpu.VMEM(shape, BF16) for shape in shapes]
+
+    units = 8
     return pl.pallas_call(
-        functools.partial(backward_kernel, tasks, by_rows),
-        grid=(8,),
+        functools.partial(back_kernel, n_dp),
+        grid=(2 * units,),
         out_shape=[
-            jax.ShapeDtypeStruct((8, 256, 768), BF16),
-            jax.ShapeDtypeStruct(dx, BF16),
-            jax.ShapeDtypeStruct(gate.shape, F32),
-            jax.ShapeDtypeStruct((256, 128), F32),
+            jax.ShapeDtypeStruct((units, 2, 4, 16, 768) if full else (units, 2, 2, 2, 2, 16, 768), BF16),
+            jax.ShapeDtypeStruct((4, 2, 4, 16, 256) if full else (1, 2, 2, 2, 16, 256), BF16),
+            jax.ShapeDtypeStruct((4, total, 128), BF16),
+            jax.ShapeDtypeStruct((4,) + req.shape, F32),
+            jax.ShapeDtypeStruct((3, rows), F32),
         ],
         in_specs=[
-            pl.BlockSpec(x_t.shape, lambda e: (0, 0)),
-            pl.BlockSpec((4, 1, 64, wa.shape[3]), lambda e: (0, e, 0, 0)),
-            pl.BlockSpec(gate.shape, lambda e: (0, 0)),
-            pl.BlockSpec(g.shape, lambda e: (0, 0, 0)),
-            pl.BlockSpec(dz.shape, lambda e: (0, 0)),
-            per, per, per,
-        ],
-        out_specs=[
-            pl.BlockSpec((1, 256, 768), lambda e: (e, 0, 0)),
-            pl.BlockSpec(dx, lambda e: (0,) * len(dx)),
-            pl.BlockSpec(gate.shape, lambda e: (0, 0)),
-            pl.BlockSpec((256, 128), lambda e: (0, 0)),
-        ],
+            fixed(x1),
+            fixed(x2),
+            pl.BlockSpec((4, 1, 64, wa1.shape[3]), lambda i: (0, first(i), 0, 0)),
+            pl.BlockSpec((4, 1, 64, wa2.shape[3]), lambda i: (0, second(i), 0, 0)),
+            fixed(gate1), fixed(gate2), fixed(g1), fixed(g2), fixed(dz2),
+            per1, per1, per1, per2, per2, per2,
+            fixed(dtower), fixed(tsums), hbm, fixed(pred), fixed(place),
+        ],
+        out_specs=[hbm, hbm, hbm, hbm, pl.BlockSpec((3, rows), lambda i: (0, 0))],
         scratch_shapes=[
             pltpu.VMEM((512, total), F32),
-            pltpu.VMEM((tasks, 8, total), F32),
-        ],
-        compiler_params=pltpu.CompilerParams(vmem_limit_bytes=58 * MIB),
-    )(x_t, wa, gate, g, dz, h, s, y)
-
-
-UNITS = 9
-
-
-def sum_kernel(
-    n_dp, grads, dxq, req, pred, place,
-    shard, shared, dx_all, req_all, pred_out,
-    core_in, mine, y_in, half, x_in, quarter, z_in, piece, gathered, pred_send, pred_recv,
-    sem_s, sem_r, z_send, z_recv, zz_send, zz_recv, dx_send, dx_recv, rq_send, rq_recv, p_send, p_recv, loc,
-):
-    d, p, p1, p2, d1 = partners(n_dp)
-    deep = n_dp // 2
-    full = deep == 4
-    z, dx, py, pc = d // 2, d % 2, p // 2, p % 2
-    cap = pred_send.shape[2]
-    greet([((d + k) % n_dp, p) for k in range(1, n_dp)] + [(d, (p + k) % 4) for k in range(1, 4)])
-
-    back = []
-    for i in range(n_dp):
-        pred_send[i] = pred[i]
-    for k in range(1, n_dp):
-        to = (d + k) % n_dp
-        back.append(remote(pred_send.at[to], pred_recv.at[d], p_send.at[k], p_recv.at[k], (to, p)))
-        back[-1].start()
-    pred_recv[d] = pred_send[d]
-
-    moves = []
-    for k in range(1, 4):
-        to = (p + k) % 4
-        moves.append(remote(dxq.at[to], dx_all.at[p], dx_send.at[k], dx_recv.at[k], (d, to)))
-        moves.append(remote(req, req_all.at[p], rq_send.at[k], rq_recv.at[k], (d, to)))
-    keep = [
-        pltpu.make_async_copy(dxq.at[p], dx_all.at[p], loc.at[0]),
-        pltpu.make_async_copy(req, req_all.at[p], loc.at[1]),
-    ]
-
-    started = {}
-
-    def go(name, copy):
-        copy.start()
-        started.setdefault(name, []).append(copy)
-
-    def stage0(u):
-        for yy in range(2):
-            go((0, u), remote(
-                grads.at[u, :, 2 * yy + (1 - pc)], core_in.at[u, yy],
-                sem_s.at[u, yy], sem_r.at[u, yy], (d, p1)))
-
-    def stage1(u):
-        for copy in started[(0, u)]:
-            copy.wait()
-        for yy in range(2):
-            mine[u, yy] = (
-                grads[u, :, 2 * yy + pc].astype(F32) + core_in[u, yy].astype(F32)
-            ).astype(BF16)
-        go((1, u), remote(
-            mine.at[u, 1 - py], y_in.at[u], sem_s.at[u, 2], sem_r.at[u, 2], (d, p2)))
-
-    def stage2(u):
-        for copy in started[(1, u)]:
-            copy.wait()
-        total = mine[u, py].astype(F32) + y_in[u].astype(F32)
-        if not full:
-            shard[u] = total
-            return
-        for xh in range(2):
-            half[u, xh] = total[:, xh].astype(BF16)
-        go((2, u), remote(
-            half.at[u, 1 - dx], x_in.at[u], sem_s.at[u, 3], sem_r.at[u, 3], (d1, p)))
-
-    def stage3(u):
-        for copy in started[(2, u)]:
-            copy.wait()
-        quarter[u] = (half[u, dx].astype(F32) + x_in[u].astype(F32)).astype(BF16)
-        for k in range(1, 4):
-            to = (z + k) % 4
-            go((3, u), remote(
-                quarter.at[u, to // 2, to % 2], z_in.at[u, k],
-                z_send.at[u, k], z_recv.at[u, k], (2 * to + dx, p)))
-
-    def stage4(u):
-        for copy in started[(3, u)]:
-            copy.wait()
-        total = quarter[u, z // 2, z % 2].astype(F32)
-        for k in range(1, 4):
-            total = total + z_in[u, k].astype(F32)
-        piece[u] = total.astype(BF16)
-        gathered[u, dx, z] = piece[u]
-        for k in range(1, 4):
-            to = (z + k) % 4
-            go((4, u), remote(
-                piece.at[u], gathered.at[u, dx, z],
-                zz_send.at[u, k], zz_recv.at[u, k], (2 * to + dx, p)))
-
-    def stage5(u):
-        for copy in started[(4, u)]:
-            copy.wait()
-        go((5, u), remote(
-            gathered.at[u, dx], gathered.at[u, dx], sem_s.at[u, 4], sem_r.at[u, 4], (d1, p)))
-
-    def stage6(u):
-        for copy in started[(5, u)]:
-            copy.wait()
-        for xh in range(2):
-            for e in range(2):
-                for zr in range(2):
-                    shard[u, e, xh, zr] = gathered[u, xh, 2 * e + zr].astype(F32)
-
-    stages = [stage0, stage1, stage2] + ([stage3, stage4, stage5, stage6] if full else [])
-    for tick in range(UNITS + len(stages) - 1):
-        for at in range(len(stages) - 1, -1, -1):
-            u = tick - at
-            if 0 <= u < UNITS:
-                stages[at](u)
-        if tick == 1:
-            for move in moves + keep:
-                move.start()
-    last = UNITS - 1
-    if full:
-        shared[p] = gathered[last]
-        again = [
-            remote(gathered.at[last], shared.at[p], sem_s.at[k, 5], sem_r.at[k, 5], (d, (p + k) % 4))
-            for k in range(1, 4)
+            pltpu.VMEM((512, total), BF16),
+            pltpu.VMEM((3, 8, total), F32),
+            pltpu.VMEM((256, 128), F32),
+            pltpu.VMEM((40, 512), F32),
+            pltpu.VMEM((4, total, 128), BF16),
         ]
-        for copy in again:
-            copy.start()
-    else:
-        again = []
-    for copy in back:
-        copy.wait()
-    rows = place.shape[1]
-    out = jnp.zeros((16, rows), F32)
-    for i in range(n_dp):
-        c = pred_recv[i]
-        high = c.astype(BF16).astype(F32)
-        low = c - high
-        both = jnp.concatenate([high, low], axis=0).astype(BF16)
-        at = lax.broadcasted_iota(jnp.int32, (cap, rows), 0) + i * cap
-        pick = jnp.where(at == place[...], 1.0, 0.0).astype(BF16)
-        out = out + dot(both, pick)
-    pred_out[...] = (out[0:8] + out[8:16])[0:3]
-    for copy in again:
-        copy.wait()
-    for move in moves + keep:
-        move.wait()
-
-
-def sum_up(n_dp, grads, dxq, req, pred, place):
-    full = n_dp == 8
-    cap = pred.shape[2]
-    rows = place.shape[1]
-    dma = pltpu.SemaphoreType.DMA
-    vmem = pl.BlockSpec(memory_space=VMEM)
-    hbm = pl.BlockSpec(memory_space=ANY)
-    part = (2, 2, 16, 768)
-    return pl.pallas_call(
-        functools.partial(sum_kernel, n_dp),
-        out_shape=[
-            jax.ShapeDtypeStruct((UNITS, 2) + part, F32),
-            jax.ShapeDtypeStruct((4, 2, 4, 16, 768), BF16),
-            jax.ShapeDtypeStruct(dxq.shape, BF16),
-            jax.ShapeDtypeStruct((4,) + req.shape, F32),
-            jax.ShapeDtypeStruct((3, rows), F32),
-        ],
-        in_specs=[vmem, hbm, hbm, vmem, vmem],
-        out_specs=[vmem, vmem, hbm, hbm, vmem],
-        scratch_shapes=[
-            pltpu.VMEM((UNITS, 2, 2) + part, BF16),
-            pltpu.VMEM((UNITS, 2, 2) + part, BF16),
-            pltpu.VMEM((UNITS, 2) + part, BF16),
-            pltpu.VMEM((UNITS, 2, 2, 2, 16, 768), BF16),
-            pltpu.VMEM((UNITS, 2, 2, 16, 768), BF16),
-            pltpu.VMEM((UNITS, 2, 2, 16, 768), BF16),
-            pltpu.VMEM((UNITS, 4, 16, 768), BF16),
-            pltpu.VMEM((UNITS, 16, 768), BF16),
-            pltpu.VMEM((UNITS, 2, 4, 16, 768), BF16),
+        + buffers(units, 768)
+        + buffers(1, 256)
+        + [
             pltpu.VMEM((n_dp, 8, cap), F32),
             pltpu.VMEM((n_dp, 8, cap), F32),
-            dma((UNITS, 6)),
-            dma((UNITS, 6)),
-            dma((UNITS, 4)),
-            dma((UNITS, 4)),
-            dma((UNITS, 4)),
-            dma((UNITS, 4)),
+            dma((units + 1, 5)),
+            dma((units + 1, 5)),
+            dma((units + 1, 4)),
+            dma((units + 1, 4)),
+            dma((units + 1, 4)),
+            dma((units + 1, 4)),
             dma((4,)),
             dma((4,)),
             dma((4,)),
             dma((4,)),
             dma((n_dp,)),
             dma((n_dp,)),
-            dma((2,)),
+            dma((4,)),
+            dma((4,)),
+            dma((4,)),
         ],
         compiler_params=pltpu.CompilerParams(
-            collective_id=1, has_side_effects=True, vmem_limit_bytes=58 * MIB
+            collective_id=1, has_side_effects=True, vmem_limit_bytes=62 * MIB
         ),
-    )(grads, dxq, req, pred, place)
+    )(
+        x1, x2, wa1, wa2, gate1, gate2, g1, g2, dz2, *l1, *l2, dtower, tsums, req, pred, place
+    )
 
 
 def scatter_kernel(slots, dx, out, a0, a1, a2, a3, buf):
@@ -717,38 +780,27 @@
     h1, s1, y1, g1, x2 = layer_forward(x1, wa1, g1t, bo1, 2)
     h2, s2, y2, g2, zb = layer_forward(x2, wa2, g2t, bo2, 3)
     pred, dz2, dtower, tsums = towers(zb, tower_in, vec, flat)
-    grads2, dz1, dgate2, sums2 = layer_backward(x2, wa2, g2t, g2, dz2, h2, s2, y2, 3, False)
-    grads1, dxq, dgate1, sums1 = layer_backward(x1, wa1, g1t, g1, dz1, h1, s1, y1, 2, True)
-    biases = jnp.concatenate([sums1[:, :16], sums2[:, :16]], axis=1).T
-    gates = jnp.concatenate([dgate1, dgate2], axis=0)
-    small = tsums[:, :, :3].transpose(2, 0, 1).reshape(3, 384)
-    small = jnp.concatenate([small.reshape(1, -1), jnp.zeros((1, 768 * 2 - 1152), F32)], axis=1)
-    small = small.reshape(2, 768)
-    shared = jnp.concatenate(
-        [
-            dtower,
-            jnp.concatenate([gates, jnp.pad(biases, ((0, 8), (0, 0)))], axis=1),
-            small,
-            jnp.zeros((512 - 128 - 40 - 2, 768), F32),
-        ],
-        axis=0,
-    ).astype(BF16)
-    grads = jnp.concatenate([grads2, grads1, shared.reshape(2, 256, 768)], axis=0)
-    grads = grads.reshape(UNITS, 2, 4, 2, 2, 16, 768)
     by_source = pred.reshape(8, n_dp, cap).transpose(1, 0, 2)
-    sums, whole, dx_all, req_all, predictions = sum_up(n_dp, grads, dxq, req, by_source, place)
+    sums, whole, dx_all, req_all, predictions = backward(
+        n_dp, x1, x2, wa1, wa2, g1t, g2t, g1, g2, dz2, (h1, s1, y1), (h2, s2, y2),
+        dtower, tsums, req, by_source, place,
+    )
     if n_dp == 8:
-        whole = whole.reshape(4, 2, 2, 2, 16, 768).transpose(2, 0, 1, 3, 4, 5)
-        whole = whole.reshape(512, 768).astype(F32)
+        sums = sums.reshape(2, 4, 2, 2, 2, 16, 768).transpose(0, 1, 3, 2, 4, 5, 6).astype(F32)
+        whole = whole.reshape(4, 2, 2, 2, 16, 256).transpose(2, 0, 1, 3, 4, 5)
     else:
-        sums = lax.psum(sums, "dp")
-        whole = lax.all_gather(sums[UNITS - 1], "mp", axis=0)
-        whole = whole.transpose(1, 0, 2, 3, 4, 5).reshape(512, 768)
-    sums = sums[: UNITS - 1].reshape(2, 8, 64, 768)
+        sums = lax.psum(sums[:, 0].astype(F32), "dp")
+        sums = sums.reshape(2, 4, 2, 2, 2, 16, 768).transpose(0, 1, 3, 2, 4, 5, 6)
+        whole = lax.all_gather(lax.psum(whole[0].astype(F32), "dp"), "mp", axis=0)
+        whole = whole.transpose(2, 0, 1, 3, 4, 5)
+    whole = whole.reshape(512, 256).astype(F32)
+    sums = sums.reshape(2, 8, 64, 768)
     slots = req_all[:, :, 0, :].reshape(4, total).astype(jnp.int32)
     table_grad = scatter(slots, dx_all, table.shape[0])
-    dtower, gates, biases = whole[:128], whole[128:168, :512], whole[128:160, 512:]
-    small = whole[168:170].reshape(-1)[:1152].reshape(3, 3, 128)
+    dtower = whole[:384].reshape(3, 128, 256).transpose(0, 2, 1)
+    gates = jnp.concatenate([whole[384:424], whole[424:464]], axis=1)
+    biases = whole[464:496]
+    small = jnp.stack([whole[496:499, :128], whole[496:499, 128:], whole[504:507, :128]], axis=1)
     inner = w_in1.shape[2]
     start = lax.axis_index("mp") * inner
     b_in = [lax.dynamic_slice_in_dim(biases[k : k + 8], start, inner, axis=1) for k in (8, 24)]
@@ -766,7 +818,7 @@
         sums[0, :, :, 512:],
         biases[16:24],
         gates[16:40].T.reshape(gate2.shape),
-        dtower.reshape(128, 3, 256).transpose(1, 2, 0),
+        dtower,
         small[0],
         small[1],
         small[2, :, 0],

time: 325 us -> 245 us (0.75)
  Pallas kernels: 283 us -> 221 us
  local copies, waits for them, and re-layouts: 28.6 us -> 15.8 us
  other arithmetic: 10.8 us -> 5.45 us
    pallas_call x3 -> x1, Pallas kernels: 164 us -> 103 us  [backward(): pl.pallas_call(functools.partial(back_kernel, n_dp), grid=(2 * units,), o...]
    slice x11 -> x2, local copies, waits for them, and re-layouts: 8.82 us -> 0.03 us  [the longest x1 0.03 us: on_device(): dtower = whole[:384].reshape(3, 128, 256).transpose(0, 2, 1)]
    concatenate x2 -> x0, other arithmetic: 6.35 us -> none  [the longest x1 5.52 us: on_device(): jnp.concatenate([grads2, grads1, shared.reshape(2, 256, 768)], axis=0)]
where the time goes in v2:
time: 245 us; the launch traced here: 243 us
  Pallas kernels  221 us (90%)
  local copies, waits for them, and re-layouts  15.8 us (6%)
  other arithmetic  5.45 us (2%)
    pallas_call x1, Pallas kernels, backward(): pl.pallas_call(functools.partial(back_kernel, n_dp), grid=(2 * units,), o...  103 us
    pallas_call x1, Pallas kernels, fetch(): pl.pallas_call(functools.partial(fetch_kernel, n_dp, cap), out_shape=[jax...  50.7 us
    pallas_call x2, Pallas kernels, layer_forward(): pl.pallas_call(functools.partial(forward_kernel, tasks), grid=(8,), out_s...  40.4 us
    pallas_call x1, Pallas kernels, scatter(): pl.pallas_call(scatter_kernel, out_shape=jax.ShapeDtypeStruct(table, F32)...  20.1 us
    pallas_call x1, Pallas kernels, towers(): pl.pallas_call(tower_kernel, grid=(3,), out_shape=[jax.ShapeDtypeStruct((...  6.62 us

profile of v2, /device:TPU:1, one launch (start us, length us, event | category | flops | bytes accessed | tf_op | source)
XLA Modules:
  0.0 243.0 jit_solution(12927359849652429761)
XLA Ops:
  0.7 0.8 broadcast_in_dim.10
  1.5 0.8 broadcast_in_dim.11
  2.3 1.6 pad_maximum_fusion
  4.0 50.7 %shard_map.297 = (bf16[512,2048]{1,0:T(8,128)(2,1)S(1)}, f32[8,8,256]{2,1,0:T(8,128)S(1)}, s32[1,512]{1,0:T(1,128)S(1)}, bf16[4,8,64,896]{3,2,1,0:T(8,128)(2,1)}, bf16[4,8,64,896]{3,2,1,0:T(8,128)(2,1)}) custom-call(s32[1,512]{1,0:T(1,128)S(1)} %bitcast.61, s32[1,512]{1,0:T(1,128)S(1)} %bitcast.62, f32[3,512]{1,0:T(4,128)S(1)} %copy-done.2, ...), custom_call_target="tpu_custom_call" | custom-call | tf_op jit(solution)/shard_map/pallas_call | solution.py:215
  54.7 1.3 copy-done
  56.0 0.6 copy-done.1
  57.2 1.1 broadcast_in_dim.12.bo
  58.3 19.1 %shard_map.298 = (bf16[8,256,2048]{2,1,0:T(8,128)(2,1)}, bf16[8,256,2048]{2,1,0:T(8,128)(2,1)}, bf16[8,256,2048]{2,1,0:T(8,128)(2,1)}, f32[2,8,2048]{2,1,0:T(8,128)}, bf16[512,2048]{1,0:T(8,128)(2,1)}) custom-call(bf16[512,2048]{1,0:T(8,128)(2,1)} %copy-done, bf16[4,8,64,896]{3,2,1,0:T(8,128)(2,1)} %get-tuple-element.41.wa.wa1, bf16[16,512]{1,0:T(8,128)(2,1)} %bitcast.79, ...), custom_call_target="tpu_custom_call" | custom-call | tf_op jit(solution)/shard_map/pallas_call | solution.py:287
  77.5 1.1 broadcast_in_dim.13.bo
  78.6 21.2 %shard_map.299 = (bf16[8,256,2048]{2,1,0:T(8,128)(2,1)}, bf16[8,256,2048]{2,1,0:T(8,128)(2,1)}, bf16[8,256,2048]{2,1,0:T(8,128)(2,1)}, f32[3,8,2048]{2,1,0:T(8,128)}, bf16[768,2048]{1,0:T(8,128)(2,1)}) custom-call(bf16[512,2048]{1,0:T(8,128)(2,1)} %get-tuple-element.42.x_t.x2, bf16[4,8,64,896]{3,2,1,0:T(8,128)(2,1)} %get-tuple-element.43.wa.wa2, ...), custom_call_target="tpu_custom_call" | custom-call | tf_op jit(solution)/shard_map/pallas_call | solution.py:287
  100.0 0.9 broadcast_in_dim.14.vec
  100.9 6.6 %shard_map.300 = (f32[8,2048]{1,0:T(8,128)}, bf16[768,2048]{1,0:T(8,128)(2,1)}, f32[128,768]{1,0:T(8,128)}, f32[3,8,128]{2,1,0:T(8,128)}) custom-call(bf16[768,2048]{1,0:T(8,128)(2,1)} %get-tuple-element.46.zb, bf16[3,256,128]{2,1,0:T(8,128)(2,1)} %w.1, bf16[3,3,128,128]{3,2,1,0:T(8,128)(2,1)} %broadcast_in_dim.14.vec, f32[8,2048]{1,0:T(8,128)} %bitcast.60), custom_call_target="tpu_custom_call" | custom-call | tf_op jit(solution)/shard_map/pallas_call | solution.py:341
  107.5 103.1 %shard_map.301 = (bf16[8,2,4,16,768]{4,3,2,1,0:T(8,128)(2,1)}, bf16[4,2,4,16,256]{4,3,2,1,0:T(8,128)(2,1)}, bf16[4,2048,128]{2,1,0:T(8,128)(2,1)}, f32[4,8,8,256]{3,2,1,0:T(8,128)}, f32[3,512]{1,0:T(4,128)}) custom-call(bf16[512,2048]{1,0:T(8,128)(2,1)} %copy-done, bf16[512,2048]{1,0:T(8,128)(2,1)} %get-tuple-element.42.x_t.x2, ...), custom_call_target="tpu_custom_call" | custom-call | tf_op jit(solution)/shard_map/pallas_call | solution.py:646
  210.6 1.1 convert_bitcast_fusion.1
  212.4 0.6 slice_reduce_fusion
  213.1 0.6 fusion
  215.1 1.6 slice_bitcast_fusion
  216.7 1.1 slice_bitcast_fusion.2
  217.7 1.0 convert_reduce_fusion
  218.8 0.6 copy.46
  219.4 20.1 %shard_map.302 = f32[8192,128]{1,0:T(8,128)} custom-call(s32[4,2048]{1,0:T(4,128)} %bitcast.75, bf16[4,2048,128]{2,1,0:T(8,128)(2,1)} %get-tuple-element.61.dx), custom_call_target="tpu_custom_call" | custom-call | tf_op jit(solution)/shard_map/pallas_call | solution.py:732
  239.5 0.9 copy.43
  241.1 0.7 constant_dynamic-slice_fusion
  241.7 0.7 constant_dynamic-slice_fusion.1
  (41 shorter events, 3.9 us)
Async XLA Ops:
  0.6 3.3 %copy-start.4 = (s32[512,1]{0,1:T(1,128)S(1)}, s32[512,1]{0,1:T(1,128)}, u32[]{:S(2)}) copy-start(s32[512,1]{0,1:T(1,128)} %param.18) | copy-start | bytes 6148
  0.7 3.3 %copy-start.5 = (s32[512]{0:T(512)S(1)}, s32[512]{0:T(512)}, u32[]{:S(2)}) copy-start(s32[512]{0:T(512)} %param.19) | copy-start | bytes 6148
  0.7 3.3 %copy-start.2 = (f32[3,512]{1,0:T(4,128)S(1)}, f32[3,512]{1,0:T(4,128)}, u32[]{:S(2)}) copy-start(f32[3,512]{1,0:T(4,128)} %cot.1) | copy-start | bytes 18436
  4.0 53.2 %copy-start.8 = (bf16[8,256]{1,0:T(8,128)(2,1)S(1)}, bf16[8,256]{1,0:T(8,128)(2,1)}, u32[]{:S(2)}) copy-start(bf16[8,256]{1,0:T(8,128)(2,1)} %param.24) | copy-start | bytes 12292
  54.7 1.3 copy-start
  56.0 0.6 copy-start.1
  56.6 0.6 copy-start.3
  58.3 19.1 %copy-start.9 = (bf16[8,256]{1,0:T(8,128)(2,1)S(1)}, bf16[8,256]{1,0:T(8,128)(2,1)}, u32[]{:S(2)}) copy-start(bf16[8,256]{1,0:T(8,128)(2,1)} %param.29) | copy-start | bytes 12292
  78.6 21.3 %copy-start.12 = (bf16[3]{0:T(256)(128)(2,1)S(1)}, bf16[3]{0:T(256)(128)(2,1)}, u32[]{:S(2)}) copy-start(bf16[3]{0:T(256)(128)(2,1)} %param.34) | copy-start | bytes 22
  78.6 21.3 %copy-start.10 = (bf16[3,128]{1,0:T(4,128)(2,1)S(1)}, bf16[3,128]{1,0:T(4,128)(2,1)}, u32[]{:S(2)}) copy-start(bf16[3,128]{1,0:T(4,128)(2,1)} %param.33) | copy-start | bytes 2308
  78.6 21.3 %copy-start.11 = (bf16[3,128]{1,0:T(4,128)(2,1)S(1)}, bf16[3,128]{1,0:T(4,128)(2,1)}, u32[]{:S(2)}) copy-start(bf16[3,128]{1,0:T(4,128)(2,1)} %param.32) | copy-start | bytes 2308
  210.6 3.7 %copy-start.6 = (bf16[8,2,4,16,768]{4,3,2,1,0:T(8,128)(2,1)S(1)}, bf16[8,2,4,16,768]{4,3,2,1,0:T(8,128)(2,1)}, u32[]{:S(2)}) copy-start(bf16[8,2,4,16,768]{4,3,2,1,0:T(8,128)(2,1)} %get-tuple-element.62) | copy-start | bytes 4718596
  219.4 23.0 %copy-start.7 = (f32[3,512]{1,0:T(4,128)S(1)}, f32[3,512]{1,0:T(4,128)}, u32[]{:S(2)}) copy-start(f32[3,512]{1,0:T(4,128)} %get-tuple-element.97) | copy-start | bytes 18436

commit v3 on v0

v3 whole, which is shorter than its diff:
```python
import functools

import jax
import jax.numpy as jnp
from jax import lax
from jax.experimental import pallas as pl
from jax.experimental.pallas import tpu as pltpu
from jax.sharding import PartitionSpec as P

F32, BF16 = jnp.float32, jnp.bfloat16
MESH = pl.DeviceIdType.MESH
MIB = 2**20
VMEM, ANY = pltpu.VMEM, pl.ANY
NN, NT, TN = ((1,), (0,)), ((1,), (1,)), ((0,), (0,))
LAGS = {True: (0, 1, 4, 6, 8, 10, 12), False: (0, 1, 4, 6, 8, 10, 12)}


def dot(a, b, dims=NN):
    return lax.dot_general(a, b, (dims, ((), ())), preferred_element_type=F32)


def remote(src, dst, send_sem, recv_sem, device):
    return pltpu.make_async_remote_copy(
        src_ref=src,
        dst_ref=dst,
        send_sem=send_sem,
        recv_sem=recv_sem,
        device_id=device,
        device_id_type=MESH,
    )


def greet(peers):
    barrier = pltpu.get_barrier_semaphore()
    for peer in peers:
        pl.semaphore_signal(barrier, inc=1, device_id=peer, device_id_type=MESH)
    pl.semaphore_wait(barrier, len(peers))


def partners(n_dp):
    d, p = lax.axis_index("dp"), lax.axis_index("mp")
    return d, p, p + 1 - 2 * (p % 2), (p + 2) % 4, d + 1 - 2 * (d % 2)


def column(cols, at):
    lane = lax.broadcasted_iota(jnp.int32, cols.shape, 1)
    return jnp.sum(jnp.where(lane == at, cols, 0.0), axis=1, keepdims=True)


def front_kernel(
    n_dp, cap,
    owner, slot, cot, b_in1, b_in2, b_out1, b_out2, tower_bias, tower_out, tower_last, gate1, gate2, tower_w,
    ws1, ws2, table,
    x1_out, x2_out, wa_out, hsy_out, dz2_out, slots, place_out, g1, g2, pred, dtower, tsums,
    x1, x2, wa, hsy, dz2, cols, bias, send, recv, idx_s, stage, tab, xbuf, z, cot_rows,
    own_sem, core_s, core_r, y_s, y_r, x_s, x_r, near_s, near_r, late_s, late_r,
    bias_s, bias_r, rq_s, rq_r, idx_sem, tab_sem, out_sem, hsy_sem, dz_sem,
):
    d, p, p1, p2, d1 = partners(n_dp)
    rows = owner.shape[1]
    experts = ws1.shape[0]
    half = experts // 2
    dx = d % 2
    shards = (ws1, ws2)
    total = n_dp * cap

    def own_part(layer):
        return pltpu.make_async_copy(shards[layer], wa.at[layer, p], own_sem.at[layer])

    def core_part(layer):
        return remote(
            shards[layer], wa.at[layer, p], core_s.at[layer], core_r.at[layer], (d, p1)
        )

    def span_of(side, chunk):
        return pl.ds(half * side + half // 2 * chunk, half // 2)

    def y_part(layer, c):
        at = span_of(dx, c)
        return remote(
            shards[layer].at[at], wa.at[layer, p, at], y_s.at[layer, c], y_r.at[layer, c], (d, p2)
        )

    def onward(side, c, layer, sems, device):
        part = wa.at[layer, p2, span_of(side, c)]
        return remote(part, part, sems[0].at[layer, c], sems[1].at[layer, c], device)

    def x_part(layer, c):
        return onward(dx, c, layer, (x_s, x_r), (d1, p))

    def near_part(layer, c):
        return onward(dx, c, layer, (near_s, near_r), (d, p1))

    def late_part(layer, c):
        return onward(1 - dx, c, layer, (late_s, late_r), (d, p1))

    def bias_parts():
        return [
            remote(bias.at[p], bias.at[p], bias_s.at[k], bias_r.at[k], (d, (p + k) % 4))
            for k in range(1, 4)
        ]

    def forward_on(layer, c):
        y_part(layer, c).wait_recv()
        x_part(layer, c).start()
        near_part(layer, c).start()

    def finish_on(layer, c):
        x_part(layer, c).wait_recv()
        late_part(layer, c).start()

    def arrived(layer):
        own_part(layer).wait()
        core_part(layer).wait_recv()
        for c in range(2):
            near_part(layer, c).wait_recv()
            late_part(layer, c).wait_recv()

    def sent(layer):
        core_part(layer).wait_send()
        for c in range(2):
            for part in (y_part, x_part, near_part, late_part):
                part(layer, c).wait_send()

    def gather_all():
        step = stage.shape[1]
        blocks = table.shape[0] // step

        def load(b):
            return pltpu.make_async_copy(
                table.at[pl.ds(b * step, step)], stage.at[b % 2], tab_sem.at[b % 2]
            )

        for b in range(min(2, blocks)):
            load(b).start()
        greet(
            [((d + k) % n_dp, p) for k in range(1, n_dp)]
            + [(d, (p + k) % 4) for k in range(1, 4)]
        )
        for c in range(2):
            y_part(0, c).start()
        core_part(0).start()
        own_part(0).start()
        def as_columns(parts, wide):
            both = jnp.concatenate([part[...].astype(F32) for part in parts], axis=0)
            high = both.shape[0]
            both = jnp.concatenate([both, jnp.zeros((128 - high, both.shape[1]), F32)], axis=0)
            if both.shape[1] < wide:
                both = jnp.concatenate([both, jnp.zeros((128, wide - both.shape[1]), F32)], axis=1)
            return both.T

        bias[p] = as_columns([b_in1, b_in2], 128)[0:64]
        for copy in bias_parts():
            copy.start()
        cols[0:256] = as_columns([b_out1, b_out2], 256)
        lane = lax.broadcasted_iota(jnp.int32, (3, 128), 0)
        last = tower_last[...].astype(F32)
        spread = jnp.zeros((3, 128), F32)
        for t in range(3):
            spread = jnp.where(lane == t, last[:, t : t + 1], spread)
        vectors = [tower_bias[...].astype(F32), tower_out[...].astype(F32), spread]
        cols[256:384] = as_columns(vectors, 128)

        own_row = owner[...]
        count = max(8, n_dp)
        ks = lax.broadcasted_iota(jnp.int32, (count, rows), 0)
        onehot = jnp.where(ks == own_row, 1.0, 0.0)
        upper = jnp.where(
            lax.broadcasted_iota(jnp.int32, (rows, rows), 0)
            < lax.broadcasted_iota(jnp.int32, (rows, rows), 1),
            1.0,
            0.0,
        ).astype(BF16)
        before = dot(onehot.astype(BF16), upper)
        rank = jnp.sum(before * onehot, axis=0, keepdims=True).astype(jnp.int32)
        place = own_row * cap + rank
        place_out[...] = place
        wanted = slot[...]
        c = cot[...]
        high = c.astype(BF16).astype(F32)
        mid = (c - high).astype(BF16).astype(F32)
        payload = jnp.concatenate(
            [
                (wanted // 128).astype(F32),
                (wanted % 128).astype(F32),
                high,
                mid,
                c - high - mid,
                jnp.zeros((16 - 11, rows), F32),
            ],
            axis=0,
        ).astype(BF16)
        for k in range(n_dp):
            at = lax.broadcasted_iota(jnp.int32, (cap, rows), 0) + k * cap
            pick = jnp.where(at == place, 1.0, 0.0).astype(BF16)
            got = dot(payload, pick, NT)
            send[k] = jnp.concatenate(
                [
                    got[0:1] * 128.0 + got[1:2],
                    got[2:5] + got[5:8] + got[8:11],
                    jnp.zeros((4, cap), F32),
                ],
                axis=0,
            )
        asks = [
            remote(
                send.at[(d + k) % n_dp], recv.at[d], rq_s.at[k], rq_r.at[k], ((d + k) % n_dp, p)
            )
            for k in range(1, n_dp)
        ]
        for ask in asks:
            ask.start()
        recv[d] = send[d]
        core_part(1).start()
        own_part(1).start()

        def widen(b, carry):
            load(b).wait()
            tab[pl.ds(pl.multiple_of(b * step, step), step), :] = stage[b % 2].astype(F32)

            @pl.when(b + 2 < blocks)
            def _():
                load(b + 2).start()

            return carry

        forward_on(0, 0)
        lax.fori_loop(0, blocks, widen, 0)
        forward_on(0, 1)
        for c in range(2):
            y_part(1, c).start()
        for ask in asks:
            ask.wait()
        for i in range(n_dp):
            got = recv[i]
            slots[i : i + 1, :] = jnp.clip(got[0:1].astype(jnp.int32), 0, table.shape[0] - 1)
            cot_rows[:, i * cap : (i + 1) * cap] = got
        to_smem = pltpu.make_async_copy(slots, idx_s, idx_sem)
        to_smem.start()
        to_smem.wait()

        span = xbuf.shape[0]
        for j in range(total // span):

            for i in range(span // cap):

                def fill(o, carry, i=i, j=j):
                    into = xbuf.at[pl.ds(pl.multiple_of(i * cap + o * 16, 16), 16)]
                    for u in range(16):
                        at = idx_s[j * (span // cap) + i, o * 16 + u]
                        into[u : u + 1, :] = tab[pl.ds(at, 1), :]
                    return carry

                lax.fori_loop(0, cap // 16, fill, 0)
            x1[:, j * span : (j + 1) * span] = xbuf[...].T.astype(BF16)
        for c in range(2):
            finish_on(0, c)
        arrived(0)
        for copy in bias_parts():
            copy.wait()

    def begin(tasks, x_t, gate, g):
        z[...] = jnp.zeros_like(z)
        logits = dot(gate[...], x_t[...])
        for t in range(tasks):
            part = logits[8 * t : 8 * t + 8]
            top = jnp.exp(part - jnp.max(part, axis=0, keepdims=True))
            g[t] = top / jnp.sum(top, axis=0, keepdims=True)

    def hsy_part(n):
        return pltpu.make_async_copy(hsy.at[n % 2], hsy_out.at[n], hsy_sem.at[n % 2])

    def expert(layer, tasks, e, x_t, g):
        n = experts * layer + e
        at = n % 2
        block = wa[layer, :, e].reshape(256, wa.shape[-1])
        both = bias[...].reshape(256, 128)
        pre = dot(block[:, :512], x_t[...]) + column(both, 8 * layer + e)
        u = pre * 0.5
        th = jnp.tanh(u)
        a = 1.0 + th
        smooth = u * a
        hb = smooth.astype(BF16)
        hsy[at, 0] = hb
        hsy[at, 1] = (0.5 * (a + smooth * (1.0 - th))).astype(BF16)
        ye = dot(block[:, 512:768], hb, TN) + column(cols[0:256], 8 * layer + e)
        hsy[at, 2] = ye.astype(BF16)

        for t in range(tasks):
            z[t] += g[t, pl.ds(e, 1), :] * ye
        hsy_part(n).start()

    def out_part(k):
        src = (x1, x2, wa.at[0], wa.at[1])[k]
        dst = (x1_out, x2_out, wa_out.at[0], wa_out.at[1])[k]
        return pltpu.make_async_copy(src, dst, out_sem.at[k])

    def dz_part(t):
        at = pl.ds(256 * t, 256)
        return pltpu.make_async_copy(dz2.at[at], dz2_out.at[at], dz_sem.at[t])

    gather_all()
    begin(2, x1, gate1, g1)
    out_part(0).start()
    out_part(2).start()

    def first_layer(e, carry):
        @pl.when(e >= 2)
        def _():
            hsy_part(e - 2).wait()

        expert(0, 2, e, x1, g1)
        for c in range(2):

            @pl.when(e == c)
            def _(c=c):
                forward_on(1, c)

            @pl.when(e == 4 + c)
            def _(c=c):
                finish_on(1, c)

        return carry

    lax.fori_loop(0, experts, first_layer, 0)
    for t in range(2):
        x2[256 * t : 256 * t + 256, :] = z[t].astype(BF16)
    out_part(1).start()
    arrived(1)
    out_part(3).start()
    begin(3, x2, gate2, g2)

    def second_layer(e, carry):
        hsy_part(experts + e - 2).wait()
        expert(1, 3, e, x2, g2)
        return carry

    lax.fori_loop(0, experts, second_layer, 0)
    for t in range(3):
        vec = cols[256:384]
        zt, wt = z[t].astype(BF16), tower_w[t]
        act = dot(wt, zt, TN) + column(vec, t)
        out_w = column(vec, t + 3)
        sig = 0.5 + 0.5 * jnp.tanh(0.5 * act)
        smooth = act * sig
        logit = jnp.sum(smooth * out_w, axis=0, keepdims=True) + column(vec, t + 6)[0:1]
        prob = jax.nn.sigmoid(logit)
        for i in range(n_dp):
            pred[i, t : t + 1, :] = prob[:, i * cap : (i + 1) * cap]
        dlogit = cot_rows[t + 1 : t + 2, :] * prob * (1.0 - prob)
        dact = dlogit * out_w * (sig + smooth * (1.0 - sig))
        dab = dact.astype(BF16)
        dz2[256 * t : 256 * t + 256, :] = dot(wt, dab).astype(BF16)
        dz_part(t).start()
        dtower[:, 256 * t : 256 * t + 256] = dot(dab, zt, NT)
        lane = lax.broadcasted_iota(jnp.int32, (128, 128), 1)
        one = jnp.sum(dact, axis=1, keepdims=True)
        two = jnp.sum(dlogit * smooth, axis=1, keepdims=True)
        three = jnp.sum(dlogit, axis=1, keepdims=True)
        both = jnp.where(lane == 0, one, jnp.where(lane == 1, two, three))
        tsums[t] = both.T[0:8]
    for layer in range(2):
        sent(layer)
    for n in (2 * experts - 2, 2 * experts - 1):
        hsy_part(n).wait()
    for k in range(4):
        out_part(k).wait()
    for t in range(3):
        dz_part(t).wait()


def front(n_dp, cap, small, ws1, ws2, table):
    rows, width = small[0].shape[1], table.shape[1]
    total = n_dp * cap
    step = min(1024, table.shape[0])
    whole = (4,) + ws1.shape
    dma = pltpu.SemaphoreType.DMA
    hbm = pl.BlockSpec(memory_space=ANY)
    vmem = pl.BlockSpec(memory_space=VMEM)
    shapes = [
        ((width, total), BF16),
        ((512, total), BF16),
        ((2,) + whole, BF16),
        ((16, 3, 256, total), BF16),
        ((768, total), BF16),
        ((n_dp, cap), jnp.int32),
        ((1, rows), jnp.int32),
        ((2, 8, total), F32),
        ((3, 8, total), F32),
        ((n_dp, 8, cap), F32),
        ((128, 768), F32),
        ((3, 8, 128), F32),
    ]
    return pl.pallas_call(
        functools.partial(front_kernel, n_dp, cap),
        out_shape=[jax.ShapeDtypeStruct(*s) for s in shapes],
        in_specs=[vmem] * len(small) + [hbm] * 3,
        out_specs=[hbm] * 5 + [vmem] * 7,
        scratch_shapes=[
            pltpu.VMEM((width, total), BF16),
            pltpu.VMEM((512, total), BF16),
            pltpu.VMEM((2,) + whole, BF16),
            pltpu.VMEM((2, 3, 256, total), BF16),
            pltpu.VMEM((768, total), BF16),
            pltpu.VMEM((384, 128), F32),
            pltpu.VMEM((4, 64, 128), F32),
            pltpu.VMEM((n_dp, 8, cap), F32),
            pltpu.VMEM((n_dp, 8, cap), F32),
            pltpu.SMEM((n_dp, cap), jnp.int32),
            pltpu.VMEM((2, step, width), BF16),
            pltpu.VMEM((table.shape[0], width), F32),
            pltpu.VMEM((max(256, cap), width), F32),
            pltpu.VMEM((3, 256, total), F32),
            pltpu.VMEM((8, total), F32),
            dma((2,)),
            dma((2,)),
            dma((2,)),
        ]
        + [dma((2, 2))] * 8
        + [dma((4,)), dma((4,)), dma((n_dp,)), dma((n_dp,)), dma, dma((2,))]
        + [dma((4,)), dma((2,)), dma((3,))],
        compiler_params=pltpu.CompilerParams(
            collective_id=0, has_side_effects=True, vmem_limit_bytes=62 * MIB
        ),
    )(*small, ws1, ws2, table)


def back_kernel(
    n_dp, gate1, gate2, g1, g2, dtower, tsums, pred, place, x1_in, x2_in, wa_in, dz2_in, hsy_in, slots,
    pred_out, summed, shared, dx_all, slots_all,
    x1, x2, wa, dz2, hsy, dpre_all, dz1, dg, sums, dgate, dxq, *rest,
):
    main, small, links = rest[:10], rest[10:20], rest[20:]
    pred_send, pred_recv = links[:2]
    (
        sem_s, sem_r, z_s, z_r, zz_s, zz_r, dx_s, dx_r, rq_s, rq_r, p_s, p_r, again_s, again_r, loc,
        in_sem, hsy_sem,
    ) = links[2:]
    d, p, p1, p2, d1 = partners(n_dp)
    full = n_dp == 8
    z, dx, py, pc = d // 2, d % 2, p // 2, p % 2
    cap = pred_send.shape[2]
    grads = main[0]
    units = grads.shape[0]

    def bufs_of(u):
        return (main, u) if u < units else (small, 0)

    def y_first(u):
        return u < units // 2 or not full

    def copies(stage, u):
        bufs, i = bufs_of(u)
        own, core_in, mine, one_in, half, two_in, quarter, z_in, piece, gathered = bufs
        over_y, over_x = (d, p2), (d1, p)
        if stage == 0:
            return [
                remote(
                    own.at[i, :, 2 * yy + (1 - pc)], core_in.at[i, yy],
                    sem_s.at[u, yy], sem_r.at[u, yy], (d, p1),
                )
                for yy in range(2)
            ]
        if stage == 1:
            if y_first(u):
                src, device = mine.at[i, 1 - py], over_y
            else:
                src, device = mine.at[i, :, :, 1 - dx], over_x
            return [remote(src, one_in.at[i], sem_s.at[u, 2], sem_r.at[u, 2], device)]
        if stage == 2:
            src, device = (1 - dx, over_x) if y_first(u) else (1 - py, over_y)
            return [remote(half.at[i, src], two_in.at[i], sem_s.at[u, 3], sem_r.at[u, 3], device)]
        if stage == 3:
            return [
                remote(
                    quarter.at[i, (z + k) % 4 // 2, (z + k) % 4 % 2], z_in.at[i, k],
                    z_s.at[u, k], z_r.at[u, k], (2 * ((z + k) % 4) + dx, p),
                )
                for k in range(1, 4)
            ]
        if stage == 4:
            return [
                remote(
                    piece.at[i], gathered.at[i, dx, z],
                    zz_s.at[u, k], zz_r.at[u, k], (2 * ((z + k) % 4) + dx, p),
                )
                for k in range(1, 4)
            ]
        part = gathered.at[i, dx]
        return [remote(part, part, sem_s.at[u, 4], sem_r.at[u, 4], (d1, p))]

    def advance(stage, u):
        bufs, i = bufs_of(u)
        own, core_in, mine, one_in, half, two_in, quarter, z_in, piece, gathered = bufs
        if stage:
            for copy in copies(stage - 1, u):
                copy.wait()
        if stage == 1:
            for yy in range(2):
                both = own[i, :, 2 * yy + pc].astype(F32) + core_in[i, yy].astype(F32)
                mine[i, yy] = both.astype(BF16)
        if stage == 2 and y_first(u):
            both = mine[i, py].astype(F32) + one_in[i].astype(F32)
            for xh in range(2):
                half[i, xh] = both[:, xh].astype(BF16)
        elif stage == 2:
            both = mine[i, :, :, dx].astype(F32) + one_in[i].astype(F32)
            half[i] = both.astype(BF16)
        if stage == 3:
            kept = half[i, dx if y_first(u) else py]
            quarter[i] = (kept.astype(F32) + two_in[i].astype(F32)).astype(BF16)
        if stage == 4:
            both = quarter[i, z // 2, z % 2].astype(F32)
            for k in range(1, 4):
                both = both + z_in[i, k].astype(F32)
            piece[i] = both.astype(BF16)
            gathered[i, dx, z] = piece[i]
        if stage < last_stage:
            for copy in copies(stage, u):
                copy.start()

    last_stage = 6 if full else 2

    last_step = 2 * units - 1

    def at_step(u, stage):
        whole_at = min(2 * u + 1, last_step)
        return whole_at + LAGS[y_first(u)][stage]

    def tick(at):
        for stage in range(last_stage, -1, -1):
            for u in range(units):
                if at_step(u, stage) == at:
                    advance(stage, u)

    def rounds():
        left = [
            [stage for stage in range(last_stage + 1) if at_step(u, stage) > last_step]
            for u in range(units + 1)
        ]
        for turn in range(max(cuts, last_stage + 1)):
            for u in range(units + 1):
                if turn < len(left[u]):
                    advance(left[u][turn], u)
            yield turn

    def predictions_back():
        return [
            remote(
                pred_send.at[(d + k) % n_dp], pred_recv.at[d], p_s.at[k], p_r.at[k],
                ((d + k) % n_dp, p),
            )
            for k in range(1, n_dp)
        ]

    def slots_over():
        return [
            remote(slots, slots_all.at[p], rq_s.at[k], rq_r.at[k], (d, (p + k) % 4))
            for k in range(1, 4)
        ] + [pltpu.make_async_copy(slots, slots_all.at[p], loc.at[1])]

    cut = 512
    cuts = x1.shape[1] // cut

    def columns_over(c):
        rows = pl.ds(c * cut, cut)
        return [
            remote(
                dxq.at[(p + k) % 4, rows], dx_all.at[p, rows],
                dx_s.at[c, k], dx_r.at[c, k], (d, (p + k) % 4),
            )
            for k in range(1, 4)
        ] + [pltpu.make_async_copy(dxq.at[p, rows], dx_all.at[p, rows], dx_s.at[c, 0])]

    def load(k):
        src = (dz2_in, x2_in, wa_in.at[1], x1_in, wa_in.at[0])[k]
        dst = (dz2, x2, wa.at[1], x1, wa.at[0])[k]
        return pltpu.make_async_copy(src, dst, in_sem.at[k])

    def hsy_load(n):
        return pltpu.make_async_copy(hsy_in.at[(n + 8) % 16], hsy.at[n % 2], hsy_sem.at[n % 2])

    hsy_load(0).start()
    for k in range(5):
        load(k).start()
    sums[...] = jnp.zeros_like(sums)
    greet(
        [((d + k) % n_dp, p) for k in range(1, n_dp)]
        + [(d, (p + k) % 4) for k in range(1, 4)]
    )
    for i in range(n_dp):
        pred_send[i] = pred[i]
    for copy in predictions_back() + slots_over():
        copy.start()
    pred_recv[d] = pred_send[d]

    def expert(layer, tasks, e, lanes, step, x_t, g, dz):
        at = step % 2
        w_out = wa[layer, :, e, :, 512:768].reshape(256, 256)
        ye = hsy[at, 2].astype(F32)
        dy = None
        for t in range(tasks):
            dzt = dz[256 * t : 256 * t + 256, :].astype(F32)
            term = g[t, pl.ds(e, 1), :] * dzt
            dy = term if dy is None else dy + term
            dg[t, pl.ds(e, 1), :] = jnp.sum(dzt * ye, axis=0, keepdims=True)
        dyb = dy.astype(BF16)
        dpre = dot(w_out, dyb) * hsy[at, 1].astype(F32)
        dpb = dpre.astype(BF16)
        dpre_all[e] = dpb
        split = (4, 2, 2, 16)
        grads[step // 2, step % 2, :, :, :, :, 0:512] = (
            dot(dpb, x_t[...], NT).astype(BF16).reshape(split + (512,))
        )
        grads[step // 2, step % 2, :, :, :, :, 512:768] = (
            dot(hsy[at, 0], dyb, NT).astype(BF16).reshape(split + (256,))
        )
        lane = lax.broadcasted_iota(jnp.int32, (256, 128), 1)
        one = jnp.sum(dy, axis=1, keepdims=True)
        two = jnp.sum(dpre, axis=1, keepdims=True)
        sums[...] += jnp.where(
            lane == lanes + e, one, jnp.where(lane == lanes + 8 + e, two, 0.0)
        )

    def gate_part(tasks, g):
        parts = []
        for t in range(tasks):
            gt, dgt = g[t], dg[t]
            parts.append(gt * (dgt - jnp.sum(gt * dgt, axis=0, keepdims=True)))
        return jnp.concatenate(parts, axis=0).astype(BF16)

    def input_grad(layer, c, gate, dlogits):
        at = slice(c * cut, (c + 1) * cut)
        w_in = wa[layer, :, :, :, 0:512].swapaxes(0, 1).reshape(2048, 512)
        part = dot(w_in, dpre_all[:, :, at].reshape(2048, cut), TN)
        return part + dot(gate[...], dlogits[:, at], TN)

    def one_step(layer, tasks, e, lanes, step, x_t, g, dz):
        hsy_load(step).wait()

        @pl.when(step < last_step)
        def _():
            hsy_load(step + 1).start()

        expert(layer, tasks, e, lanes, step, x_t, g, dz)

    def second_layer(e, carry):
        one_step(1, 3, e, 16, e, x2, g2, dz2)
        for at in range(8):

            @pl.when(e == at)
            def _(at=at):
                tick(at)

        return carry

    def first_layer(e, carry):
        one_step(0, 2, e, 0, 8 + e, x1, g1, dz1)
        for at in range(8):

            @pl.when(e == at)
            def _(at=at):
                tick(8 + at)

        return carry

    for k in range(3):
        load(k).wait()
    lax.fori_loop(0, 8, second_layer, 0)
    dlogits = gate_part(3, g2)
    dgate[16:40] = dot(dlogits, x2[...], NT)
    for c in range(cuts):
        dz1[:, c * cut : (c + 1) * cut] = input_grad(1, c, gate2, dlogits).astype(BF16)
    for k in range(3, 5):
        load(k).wait()
    lax.fori_loop(0, 8, first_layer, 0)
    dlogits = gate_part(2, g1)
    dgate[0:16] = dot(dlogits, x1[...], NT)
    own = small[0]
    block = (2, 2, 2, 16, 256)
    for t in range(3):
        tower = dtower[:, 256 * t : 256 * t + 256].astype(BF16).reshape(block)
        own[0, t // 2, 2 * (t % 2) : 2 * (t % 2) + 2] = tower
    gates = dgate[...]
    tail = jnp.concatenate(
        [
            gates[:, :256],
            gates[:, 256:],
            sums[...].T[:32],
            jnp.concatenate([tsums[0], tsums[1]], axis=1),
            jnp.concatenate([tsums[2], jnp.zeros((8, 128), F32)], axis=1),
        ],
        axis=0,
    )
    own[0, 1, 2:4] = tail.astype(BF16).reshape(block)
    advance(0, units)
    for turn in rounds():
        if turn < cuts:
            whole = input_grad(0, turn, gate1, dlogits)
            for q in range(4):
                block = whole[128 * q : 128 * q + 128, :]
                dxq[q, turn * cut : (turn + 1) * cut] = block.T.astype(BF16)
            for copy in columns_over(turn):
                copy.start()
    gathered = small[9]

    def again():
        return [
            remote(gathered.at[0], shared.at[p], again_s.at[k], again_r.at[k], (d, (p + k) % 4))
            for k in range(1, 4)
        ] + [pltpu.make_async_copy(gathered.at[0], shared.at[p], loc.at[2])]

    result = main[9] if full else main[2]
    out = pltpu.make_async_copy(result, summed, loc.at[3])
    if full:
        for copy in again():
            copy.start()
    else:
        for u in range(units):
            result[u, 0] = main[4][u].reshape(result.shape[2:])
        pltpu.make_async_copy(small[4].at[0], shared.at[0], loc.at[2]).start()
    out.start()
    for copy in predictions_back():
        copy.wait()
    rows = place.shape[1]
    got = jnp.zeros((16, rows), F32)
    for i in range(n_dp):
        c = pred_recv[i]
        high = c.astype(BF16).astype(F32)
        both = jnp.concatenate([high, c - high], axis=0).astype(BF16)
        at = lax.broadcasted_iota(jnp.int32, (cap, rows), 0) + i * cap
        pick = jnp.where(at == place[...], 1.0, 0.0).astype(BF16)
        got = got + dot(both, pick)
    pred_out[...] = (got[0:8] + got[8:16])[0:3]
    for copy in slots_over():
        copy.wait()
    for c in range(cuts):
        for copy in columns_over(c):
            copy.wait()
    if full:
        for copy in again():
            copy.wait()
    else:
        pltpu.make_async_copy(small[4].at[0], shared.at[0], loc.at[2]).wait()
    out.wait()


def backward(
    n_dp, gate1, gate2, g1, g2, dtower, tsums, pred, place, x1, x2, wa, dz2, hsy, slots
):
    total = x1.shape[1]
    cap, rows = pred.shape[2], place.shape[1]
    full = n_dp == 8
    dma = pltpu.SemaphoreType.DMA
    hbm = pl.BlockSpec(memory_space=ANY)
    vmem = pl.BlockSpec(memory_space=VMEM)

    def buffers(units, lanes):
        part = (2, 2, 2, 16, lanes)
        shapes = [
            (units, 2, 4) + part[1:],
            (units, 2) + part,
            (units, 2) + part,
            (units,) + part,
            (units, 2, 2, 2, 16, lanes),
            (units, 2, 2, 16, lanes),
            (units, 2, 2, 16, lanes),
            (units, 4, 16, lanes),
            (units, 16, lanes),
            (units, 2, 4, 16, lanes),
        ]
        return [pltpu.VMEM(shape, BF16) for shape in shapes]

    units = 8
    return pl.pallas_call(
        functools.partial(back_kernel, n_dp),
        out_shape=[
            jax.ShapeDtypeStruct((3, rows), F32),
            jax.ShapeDtypeStruct((units, 2, 4, 16, 768) if full else (units, 2, 2, 2, 2, 16, 768), BF16),
            jax.ShapeDtypeStruct((4, 2, 4, 16, 256) if full else (1, 2, 2, 2, 16, 256), BF16),
            jax.ShapeDtypeStruct((4, total, 128), BF16),
            jax.ShapeDtypeStruct((4,) + slots.shape, jnp.int32),
        ],
        in_specs=[vmem] * 8 + [hbm] * 6,
        out_specs=[vmem] + [hbm] * 4,
        scratch_shapes=[
            pltpu.VMEM(x1.shape, BF16),
            pltpu.VMEM(x2.shape, BF16),
            pltpu.VMEM(wa.shape, BF16),
            pltpu.VMEM(dz2.shape, BF16),
            pltpu.VMEM((2,) + hsy.shape[1:], BF16),
            pltpu.VMEM((8, 256, total), BF16),
            pltpu.VMEM((512, total), BF16),
            pltpu.VMEM((3, 8, total), F32),
            pltpu.VMEM((256, 128), F32),
            pltpu.VMEM((40, 512), F32),
            pltpu.VMEM((4, total, 128), BF16),
        ]
        + buffers(units, 768)
        + buffers(1, 256)
        + [
            pltpu.VMEM((n_dp, 8, cap), F32),
            pltpu.VMEM((n_dp, 8, cap), F32),
            dma((units + 1, 5)),
            dma((units + 1, 5)),
            dma((units + 1, 4)),
            dma((units + 1, 4)),
            dma((units + 1, 4)),
            dma((units + 1, 4)),
            dma((total // 512, 4)),
            dma((total // 512, 4)),
            dma((4,)),
            dma((4,)),
            dma((n_dp,)),
            dma((n_dp,)),
            dma((4,)),
            dma((4,)),
            dma((4,)),
            dma((5,)),
            dma((2,)),
        ],
        compiler_params=pltpu.CompilerParams(
            collective_id=1, has_side_effects=True, vmem_limit_bytes=62 * MIB
        ),
    )(
        gate1, gate2, g1, g2, dtower, tsums, pred, place, x1, x2, wa, dz2, hsy, slots
    )


def scatter_kernel(
    slots, shared, dx,
    out, bo1, bo2, bi1, bi2, gate1, gate2, tower, t_bias, t_out, t_last,
    a1, a2, a3, buf, work, raw, whole, dx_sem, out_sem,
):
    blocks, cap = slots.shape[1], slots.shape[2]
    parts = (raw, a1, a2, a3)

    def load(j):
        at = pl.ds(pl.multiple_of(j * cap, cap), cap)
        return pltpu.make_async_copy(dx.at[:, at], buf.at[j % 2], dx_sem.at[j % 2])

    load(0).start()
    for a in parts:
        a[...] = jnp.zeros_like(a)
    for q in range(4):
        for xh in range(2):
            for k in range(4):
                at = 256 * (k // 2) + 64 * q + 32 * xh + 16 * (k % 2)
                whole[at : at + 16] = shared[q, xh, k].astype(F32)
    for t in range(3):
        tower[t] = whole[128 * t : 128 * t + 128].T
    gate1[...] = jnp.concatenate([whole[384:400], whole[424:440]], axis=1).T
    gate2[...] = jnp.concatenate([whole[400:424], whole[440:464]], axis=1).T
    bo1[...] = whole[464:472]
    bo2[...] = whole[480:488]
    p = lax.axis_index("mp")
    for at, ref in ((472, bi1), (488, bi2)):
        rows = whole[at : at + 8]
        mine = jnp.zeros((8, 64), F32)
        for q in range(4):
            mine = jnp.where(p == q, rows[:, 64 * q : 64 * q + 64], mine)
        ref[...] = mine
    places = ((496, 0), (496, 128), (504, 0))
    for t, (row, lane) in enumerate(places):
        t_bias[t : t + 1] = whole[row : row + 1, lane : lane + 128]
        t_out[t : t + 1] = whole[row + 1 : row + 2, lane : lane + 128]
        t_last[:, t : t + 1] = whole[row + 2 : row + 3, lane : lane + 1]

    def block(j, carry):
        load(j).wait()

        @pl.when(j + 1 < blocks)
        def _():
            load(j + 1).start()

        wide = buf[j % 2].astype(F32)
        for q in range(4):
            work[q] = wide[q]

        def add(o, inner):
            some = work.at[:, pl.ds(pl.multiple_of(o * 8, 8), 8)]
            for u in range(8):
                for q in range(4):
                    to = pl.ds(slots[q, j, o * 8 + u], 1)
                    parts[q][to, :] += some[q, u : u + 1, :]
            return inner

        lax.fori_loop(0, cap // 8, add, 0)
        return carry

    lax.fori_loop(0, blocks, block, 0)
    rows = raw.shape[0]
    piece = rows // 4

    def store(k):
        at = pl.ds(k * piece, piece)
        return pltpu.make_async_copy(raw.at[at], out.at[at], out_sem.at[k])

    for k in range(4):
        at = slice(k * piece, (k + 1) * piece)
        raw[at] = (raw[at] + a1[at]) + (a2[at] + a3[at])
        store(k).start()
    for k in range(4):
        store(k).wait()


def scatter(slots, dx, shared, rows):
    vmem = pl.BlockSpec(memory_space=VMEM)
    hbm = pl.BlockSpec(memory_space=ANY)
    table = (rows, 128)
    cap = slots.shape[2]
    shapes = [
        table, (8, 256), (8, 256), (8, 64), (8, 64), (512, 16), (512, 24), (3, 256, 128),
        (3, 128), (3, 128), (1, 3),
    ]
    return pl.pallas_call(
        scatter_kernel,
        out_shape=[jax.ShapeDtypeStruct(shape, F32) for shape in shapes],
        in_specs=[pl.BlockSpec(memory_space=pltpu.SMEM), vmem, hbm],
        out_specs=[hbm] + [vmem] * (len(shapes) - 1),
        scratch_shapes=[
            pltpu.VMEM(table, F32),
            pltpu.VMEM(table, F32),
            pltpu.VMEM(table, F32),
            pltpu.VMEM((2, 4, cap, 128), BF16),
            pltpu.VMEM((4, cap, 128), F32),
            pltpu.VMEM(table, F32),
            pltpu.VMEM((512, 256), F32),
            pltpu.SemaphoreType.DMA((2,)),
            pltpu.SemaphoreType.DMA((4,)),
        ],
        compiler_params=pltpu.CompilerParams(vmem_limit_bytes=58 * MIB),
    )(slots, shared, dx)


def on_device(
    owner, slot, table, w_in1, b_in1, w_out1, b_out1, gate1,
    w_in2, b_in2, w_out2, b_out2, gate2,
    tower_in, tower_bias, tower_out, tower_out_bias, pred_cot,
):
    n_dp = lax.axis_size("dp")
    rows = owner.shape[0]
    cap = 4 * rows // n_dp
    g1t = gate1.reshape(gate1.shape[0], -1).T
    g2t = gate2.reshape(gate2.shape[0], -1).T
    ws1 = jnp.concatenate([w_in1.transpose(1, 2, 0), w_out1], axis=2)
    ws2 = jnp.concatenate([w_in2.transpose(1, 2, 0), w_out2], axis=2)
    small = (
        owner.reshape(1, rows), slot.reshape(1, rows), pred_cot, b_in1, b_in2, b_out1, b_out2,
        tower_bias, tower_out, tower_out_bias.reshape(1, 3), g1t, g2t, tower_in,
    )
    x1, x2, wa, hsy, dz2, slots, place, g1, g2, pred, dtower, tsums = front(
        n_dp, cap, small, ws1, ws2, table
    )
    predictions, sums, whole, dx_all, slots_all = backward(
        n_dp, g1t, g2t, g1, g2, dtower, tsums, pred, place, x1, x2, wa, dz2, hsy, slots
    )
    if n_dp == 8:
        sums = sums.reshape(2, 4, 2, 2, 2, 16, 768).transpose(0, 1, 3, 2, 4, 5, 6).astype(F32)
    else:
        sums = lax.psum(sums[:, 0].astype(F32), "dp")
        sums = sums.reshape(2, 4, 2, 2, 2, 16, 768).transpose(0, 1, 3, 2, 4, 5, 6)
        whole = lax.all_gather(lax.psum(whole[0].astype(F32), "dp"), "mp", axis=0)
        whole = whole.reshape(4, 2, 4, 16, 256).astype(BF16)
    sums = sums.reshape(2, 8, 64, 768)
    table_grad, bo1, bo2, bi1, bi2, dgate1, dgate2, tower, t_bias, t_out, t_last = scatter(
        slots_all, dx_all, whole, table.shape[0]
    )
    w_in = [sums[k, :, :, :512].transpose(2, 0, 1) for k in (1, 0)]
    return (
        predictions,
        table_grad,
        w_in[0],
        bi1,
        sums[1, :, :, 512:],
        bo1,
        dgate1.reshape(gate1.shape),
        w_in[1],
        bi2,
        sums[0, :, :, 512:],
        bo2,
        dgate2.reshape(gate2.shape),
        tower,
        t_bias,
        t_out,
        t_last.reshape(3),
    )


def solution(mesh):
    in_specs = (
        P(("dp", "mp"), None),
        P(("dp", "mp")),
        P("dp", None),
        P(None, None, "mp"),
        P(None, "mp"),
        P(None, "mp", None),
        P(),
        P(),
        P(None, None, "mp"),
        P(None, "mp"),
        P(None, "mp", None),
        P(),
        P(),
        P(),
        P(),
        P(),
        P(),
        P(None, ("dp", "mp")),
    )
    out_specs = (
        P(None, ("dp", "mp")),
        P("dp", "mp"),
        P(None, None, "mp"),
        P(None, "mp"),
        P(None, "mp", None),
        P(),
        P(),
        P(None, None, "mp"),
        P(None, "mp"),
        P(None, "mp", None),
        P(),
        P(),
        P(),
        P(),
        P(),
        P(),
    )
    return jax.shard_map(
        on_device, mesh=mesh, in_specs=in_specs, out_specs=out_specs, check_vma=False
    )
```

time: 889 us -> 194 us (0.22)
  waiting for transfers between devices: 652 us -> 0 us
  Pallas kernels: 0 us -> 181 us
  matrix products: 64.1 us -> 0 us
  local copies, waits for them, and re-layouts: 65 us -> 6.94 us
  other arithmetic: 39.9 us -> 4.48 us
  blocking collectives: 31.1 us -> 0 us
  starting transfers between devices: 16.8 us -> 0 us
  between operations: 14.9 us -> 0.69 us
    psum x3 -> x0, waiting for transfers between devices: 381 us -> none  [the longest x2 247 us: on_device(): lax.psum((shared_one[0], shared_one[1], shared_two[0], shared_two[1], tow...]
    reduce_scatter x5 -> x0, waiting for transfers between devices: 210 us -> none  [the longest x1 128 us: on_device(): lax.psum_scatter(table_part, 'mp', scatter_dimension=1, tiled=True)]
    pallas_call x0 -> x3, Pallas kernels: none -> 181 us  [the longest x1 93 us: backward(): pl.pallas_call(functools.partial(back_kernel, n_dp), out_shape=[jax.Shape...]
    dot_general x24 -> x0, matrix products: 56.9 us -> none  [the longest x2 11.9 us: layer_forward(): jnp.dot(inputs, w_in.reshape(width, -1), preferred_element_type=jnp.float32)]
    all_to_all x3 -> x0, waiting for transfers between devices: 37.9 us -> none  [the longest x1 30.7 us: on_device(): lax.all_to_all(served, 'dp', split_axis=0, concat_axis=0, tiled=True)]
    unnamed x16 -> x0, waiting for transfers between devices: 22.3 us -> none
    scatter-add x1 -> x0, other arithmetic: 21.7 us -> none  [on_device(): jnp.zeros((table.shape[0], width), jnp.float32).at[wanted].add(arrived)]
    unnamed x125 -> x3, local copies, waits for them, and re-layouts: 19.9 us -> 0.6 us
  transfers between devices with their start and end apart: 17 -> 0, of which waited for: 10 -> 0; matrix products, arithmetic and copies ran while one was open for 16% -> 0% of each run, Pallas kernels for 0% -> 0%
where the time goes in v3:
time: 194 us; the launch traced here: 193 us
  Pallas kernels  181 us (93%)
  local copies, waits for them, and re-layouts  6.94 us (4%)
  other arithmetic  4.48 us (2%)
    pallas_call x1, Pallas kernels, backward(): pl.pallas_call(functools.partial(back_kernel, n_dp), out_shape=[jax.Shape...  93 us
    pallas_call x1, Pallas kernels, front(): pl.pallas_call(functools.partial(front_kernel, n_dp, cap), out_shape=[jax...  66.4 us
    pallas_call x1, Pallas kernels, scatter(): pl.pallas_call(scatter_kernel, out_shape=[jax.ShapeDtypeStruct(shape, F32...  21.9 us

profile of v3, /device:TPU:1, one launch (start us, length us, event | category | flops | bytes accessed | tf_op | source)
XLA Modules:
  0.0 193.3 jit_solution(11867660613827199543)
XLA Ops:
  0.6 2.6 %pad_maximum_fusion = (bf16[8,64,768]{2,1,0:T(8,128)(2,1)}, bf16[8,64,768]{2,1,0:T(8,128)(2,1)}) fusion(bf16[8,64,256]{2,1,0:T(8,128)(2,1)} %param.23, bf16[8,64,512]{2,1,0:T(8,128)(2,1)} %bitcast.34, bf16[8,64,256]{2,1,0:T(8,128)(2,1)} %param.28, bf16[8,64,512]{2,1,0:T(8,128)(2,1)} %bitcast.35), kind=kLoop, calls=%fused_computation.3 | loop fusion | flops 3145728 | bytes 3145728 | tf_op jit(solution)/shard_map/concatenate | solution.py:946
  3.3 66.4 %shard_map.297 = (bf16[512,2048]{1,0:T(8,128)(2,1)}, bf16[512,2048]{1,0:T(8,128)(2,1)}, bf16[2,4,8,64,768]{4,3,2,1,0:T(8,128)(2,1)}, bf16[16,3,256,2048]{3,2,1,0...) custom-call(s32[1,512]{1,0:T(1,128)} %bitcast.42, ...), custom_call_target="tpu_custom_call" | custom-call | tf_op jit(solution)/shard_map/pallas_call | solution.py:394
  69.7 93.0 %shard_map.298 = (f32[3,512]{1,0:T(4,128)}, bf16[8,2,4,16,768]{4,3,2,1,0:T(8,128)(2,1)}, bf16[4,2,4,16,256]{4,3,2,1,0:T(8,128)(2,1)}, bf16[4,2048,128]{2,1,0:T(8,128)(2,1)}, s32[4,8,256]{2,1,0:T(8,128)}) custom-call(bf16[16,512]{1,0:T(8,128)(2,1)} %bitcast.39, bf16[24,512]{1,0:T(8,128)(2,1)} %bitcast.37, f32[2,8,2048]{2,1,0:T(8,128)} %get-tuple-element.44.g1, ...), custom_call_target="tpu_custom_call" | custom-call | tf_op jit(solution)/shard_map/pallas_call | solution.py:775
  162.6 1.8 convert_bitcast_fusion
  164.5 0.3 copy.37
  164.8 1.1 slice_bitcast_fusion.2
  165.9 1.6 slice_bitcast_fusion
  167.5 0.0 copy-start
  167.5 21.9 %shard_map.299 = (f32[8192,128]{1,0:T(8,128)}, f32[8,256]{1,0:T(8,128)}, f32[8,256]{1,0:T(8,128)}, f32[8,64]{1,0:T(8,128)}, f32[8,64]{1,0:T(8,128)}, /*index=5*/...) custom-call(s32[4,8,256]{2,1,0:T(8,128)} %get-tuple-element.57.slots, ...), custom_call_target="tpu_custom_call" | custom-call | tf_op jit(solution)/shard_map/pallas_call | solution.py:916
  189.3 1.7 copy.38
  191.0 1.7 copy.39
  192.7 0.0 copy-done
  192.7 0.6 copy.41
Async XLA Ops:
  167.5 25.2 %copy-start = (f32[3,512]{1,0:T(4,128)S(1)}, f32[3,512]{1,0:T(4,128)}, u32[]{:S(2)}) copy-start(f32[3,512]{1,0:T(4,128)} %get-tuple-element.110) | copy-start | bytes 18436
